TPU v7x, 32 devices: a whole 2x2x4 slice. The times are simulated.
32 devices in a mesh: sp: 16 (over z, x, core), hd: 2 (over y).
Axes of the slice: x: 2, y: 2, z: 4, core: 2. Of those that a mesh axis runs over, the one named last changes fastest.
Arguments:
- stream: bfloat16 [3, 2, 16, 5120], P(None, 'hd', 'sp'), may hold values from -6 to 6
- queries: bfloat16 [3, 2, 16, 5120], P(None, None, 'sp', 'hd'), may hold values from -40 to 40
- span_k: bfloat16 [3, 2, 16, 5120], P(None, None, 'sp', 'hd'), may hold values from -40 to 40
- span_v: bfloat16 [3, 2, 16, 5120], P(None, None, 'sp', 'hd'), may hold values from -6 to 6
- cache_k: bfloat16 [1536, 5120], P('sp', 'hd'), may hold values from -6 to 6
- cache_v: bfloat16 [1536, 5120], P('sp', 'hd'), may hold values from -6 to 6
- cache_age: int32 [1536], P('sp'), may hold values from 0 to 20, as said below
- history: int32 [1], replicated, may hold values from 1 to 20
- out_weight: bfloat16 [5120, 5120], P('hd', 'sp'), may hold values from -2 to 2
- attn_gate: float32 [5120], replicated, may hold values from 0.5 to 1.5
- head_shift: float32 [5120], replicated, may hold values from -3 to 3
- head_scale: float32 [5120], replicated, may hold values from -1.75 to 1.75
- head_weight: bfloat16 [5120, 64], replicated, may hold values from -0.078125 to 0.078125
- latent_cache: bfloat16 [2, 4, 32, 16], P(None, 'hd', 'sp'), may hold values from -6 to 6
- conv_weight: bfloat16 [432, 384], replicated, may hold values from -0.3125 to 0.3125
- rms_gain: float32 [384], replicated, may hold values from 0.25 to 1.75
Outputs:
- stream_out: bfloat16 [3, 2, 16, 5120], P(None, 'hd', 'sp')
- decoded: bfloat16 [3, 4, 32, 384], P(None, 'hd', 'sp')
Inputs may be any that keep to these rules, and one draw needn't show every extreme that they name: `cache_age`: 20 marks an empty cache slot. Among the 96 slots of each index of sp the live ones come first and number at least 24; some index of sp has all its slots live.
All inputs are finite; a program needn't handle non-finite values.
Results may differ from a plain program's by a relative error of at most 0.017.
Values may be sent and summed in bfloat16 or wider, within the bound.
A program may use at most 64 MiB of HBM per device.

v0:
```python
import math

import jax
import jax.numpy as jnp
from jax import lax
from jax.sharding import PartitionSpec as P

HDIM = 128
LAT = 16
PATCH = 2


def padded_2(cells, sides, width):
    for axis, dim in sides:
        count = lax.axis_size(axis)
        ends = count - 1
        head = lax.slice_in_dim(cells, 0, width, axis=dim)
        tail = lax.slice_in_dim(cells, cells.shape[dim] - width, cells.shape[dim], axis=dim)
        cells = jnp.concatenate(
            [
                lax.ppermute(tail, axis, [(i, (i + 1) % count) for i in range(ends)]),
                cells,
                lax.ppermute(head, axis, [((i + 1) % count, i) for i in range(ends)]),
            ],
            axis=dim,
        )
    return cells


def head_partials(head_index, all_queries, all_keys, all_values, is_valid):
    offset = head_index * HDIM
    query_part = lax.dynamic_slice_in_dim(all_queries, offset, HDIM, 1)
    key_part = lax.dynamic_slice_in_dim(all_keys, offset, HDIM, 1)
    value_part = lax.dynamic_slice_in_dim(all_values, offset, HDIM, 1)
    scores = lax.dot_general(
        query_part, key_part, (((1,), (1,)), ((), ())), preferred_element_type=jnp.float32
    )
    scores = jnp.where(is_valid[None, :], scores * (1.0 / math.sqrt(HDIM)), -1e30)
    top_score = jnp.max(scores, axis=1)
    weights = jnp.exp(scores - top_score[:, None]).astype(jnp.bfloat16)
    weight_sum = jnp.sum(weights.astype(jnp.float32), axis=1)
    summed = jnp.dot(weights, value_part, preferred_element_type=jnp.float32)
    return (top_score, weight_sum, summed)


def settle(incoming):
    top_score, weight_sum, summed = incoming
    peak_score = jnp.max(top_score, axis=4, keepdims=True)
    factor = jnp.exp(top_score - peak_score)
    denominator = jnp.sum(weight_sum * factor, axis=4)
    numerator = jnp.sum(summed * factor[..., None], axis=4)
    return numerator / denominator[..., None]


def causal_conv(padded, frames, height, breadth, conv_weight, rms_gain):
    tap_list = []
    for step_t in range(3):
        for step_i in range(3):
            for step_j in range(3):
                tap_list.append(
                    padded[
                        step_t : step_t + frames,
                        step_i : step_i + height,
                        step_j : step_j + breadth,
                        :,
                    ]
                )
    patches = jnp.concatenate(tap_list, axis=-1)
    conv_out = jnp.dot(
        patches.reshape(-1, patches.shape[-1]), conv_weight, preferred_element_type=jnp.float32
    )
    mean_square = jnp.mean(conv_out * conv_out, axis=-1, keepdims=True)
    scaled = conv_out * lax.rsqrt(mean_square + 1e-06) * rms_gain
    return jax.nn.silu(scaled).astype(jnp.bfloat16).reshape(frames, height, breadth, -1)


def local(
    stream,
    queries,
    span_k,
    span_v,
    cache_k,
    cache_v,
    cache_age,
    history,
    out_weight,
    attn_gate,
    head_shift,
    head_scale,
    head_weight,
    latent_cache,
    conv_weight,
    rms_gain,
):
    frames = queries.shape[0]
    row_total = queries.shape[1]
    local_d = queries.shape[3]
    head_count = local_d // HDIM
    gathered = lax.all_gather(queries, "sp", axis=2, tiled=True)
    col_total = gathered.shape[2]
    all_queries = gathered.reshape(-1, local_d)
    all_keys = jnp.concatenate([cache_k, span_k.reshape(-1, local_d)], axis=0)
    all_values = jnp.concatenate([cache_v, span_v.reshape(-1, local_d)], axis=0)
    is_valid = jnp.concatenate([cache_age < history[0], jnp.ones((frames * row_total,), jnp.bool_)])

    def one_head(head_index):
        return head_partials(head_index, all_queries, all_keys, all_values, is_valid)

    top_score, weight_sum, summed = lax.map(one_head, jnp.arange(head_count, dtype=jnp.int32))
    top_parts = top_score.reshape(head_count, frames, row_total, col_total, 1)
    sum_parts = weight_sum.reshape(head_count, frames, row_total, col_total, 1)
    out_parts = summed.reshape(head_count, frames, row_total, col_total, 1, HDIM)
    attended_f = settle(
        (
            lax.all_to_all(top_parts, "sp", split_axis=3, concat_axis=4, tiled=True),
            lax.all_to_all(sum_parts, "sp", split_axis=3, concat_axis=4, tiled=True),
            lax.all_to_all(out_parts, "sp", split_axis=3, concat_axis=4, tiled=True),
        )
    )
    attended = (
        jnp.transpose(attended_f, (1, 2, 3, 0, 4))
        .reshape(frames, row_total, 1, local_d)
        .astype(jnp.bfloat16)
    )
    spread = jnp.einsum(
        "frcd,de->frce",
        lax.all_gather(attended, "sp", axis=2, tiled=True),
        out_weight,
        preferred_element_type=jnp.float32,
    )
    head_terms = lax.psum_scatter(
        spread.astype(jnp.bfloat16), "hd", scatter_dimension=1, tiled=True
    ).astype(jnp.float32)
    projected = lax.all_to_all(
        head_terms.astype(jnp.bfloat16), "sp", split_axis=2, concat_axis=3, tiled=True
    ).astype(head_terms.dtype)
    stream_out = (stream.astype(jnp.float32) + attn_gate * projected).astype(jnp.bfloat16)
    mixed_f = stream_out.astype(jnp.float32)
    centre_mean = jnp.mean(mixed_f, axis=-1, keepdims=True)
    centred = mixed_f - centre_mean
    variance = jnp.mean(centred * centred, axis=-1, keepdims=True)
    normed = (centred * lax.rsqrt(variance + 1e-06) * (1.0 + head_scale) + head_shift).astype(
        jnp.bfloat16
    )
    own_count = normed.shape[1]
    patch_values = jnp.dot(
        normed.reshape(-1, normed.shape[3]), head_weight, preferred_element_type=jnp.float32
    ).astype(jnp.bfloat16)
    patch_values = patch_values.reshape(frames, own_count, 1, PATCH, PATCH, LAT)
    latent = jnp.transpose(patch_values, (0, 1, 3, 2, 4, 5)).reshape(
        frames, own_count * PATCH, PATCH, LAT
    )
    sequence = jnp.concatenate([latent_cache, latent], axis=0)
    padded = padded_2(sequence, (("sp", 2), ("hd", 1)), 1)
    decoded = causal_conv(padded, frames, own_count * PATCH, PATCH, conv_weight, rms_gain)
    return (stream_out, decoded)


def solution(mesh):
    placed = (
        P(None, "hd", "sp", None),
        P(None, None, "sp", "hd"),
        P(None, None, "sp", "hd"),
        P(None, None, "sp", "hd"),
        P("sp", "hd"),
        P("sp", "hd"),
        P("sp"),
        P(),
        P("hd", "sp"),
        P(),
        P(),
        P(),
        P(),
        P(None, "hd", "sp", None),
        P(),
        P(),
    )
    return jax.shard_map(
        local,
        mesh=mesh,
        in_specs=placed,
        out_specs=(P(None, "hd", "sp", None), P(None, "hd", "sp", None)),
        check_vma=False,
    )
```

profile of v0, /device:TPU:1, one launch (start us, length us, event | category | flops | bytes accessed | tf_op | source)
XLA Modules:
  0.0 209.1 jit_solution(7245689909447603290)
XLA Ops:
  2.3 24.6 %all_gather.6 = bf16[3,2,16,2560]{3,1,2,0:T(2,128)(2,1)S(1)} all-gather(bf16[3,2,1,2560]{3,1,2,0:T(2,128)(2,1)} %param.19), channel_id=1, replica_groups=mesh['sp'=16,'hd'=2] {'sp'}, dimensions={2}, use_global_device_ids=true | all-gather | bytes 522240 | tf_op jit(solution)/shard_map/all_gather | solution.py:99
  28.4 2.0 pad_maximum_fusion
  30.5 69.4 %while.14 = (s32[]{:T(128)}, f32[20,96]{1,0:T(8,128)S(1)}, f32[20,96]{1,0:T(8,128)S(1)}, f32[20,96,128]{2,1,0:T(8,128)S(1)}, pred[102]{0:T(512)(128)(4,1)S(1)}, ...) while((s32[]{:T(128)}, f32[20,96]{1,0:T(8,128)S(1)}, ...), condition=%wide.region_3.4_spmd, body=%wide.region_0.3_spmd.sunk | while | flops 5101446 | bytes 259907 | solution.py:109
  42.1 1.0 fusion.38
  45.6 1.0 fusion.38
  76.8 1.0 fusion.38
  100.7 3.4 %all-to-all-start.1 = ((f32[20,3,2,16,1]{0,2,4,1,3:T(2,128)}), f32[20,3,2,16,1]{0,2,4,1,3:T(2,128)S(1)}, u32[]{:S(2)}, u32[]{:S(2)}) async-start(f32[20,3,2,16,1]{0,2,4,1,3:T(2,128)} %copy.68), calls=%async_computation.1 | async-start | bytes 98304 | tf_op jit(solution)/shard_map/all_to_all | solution.py:115
  105.0 5.2 %all-to-all-done.1 = f32[20,3,2,16,1]{0,2,4,1,3:T(2,128)S(1)} async-done(((f32[20,3,2,16,1]{0,2,4,1,3:T(2,128)}), f32[20,3,2,16,1]{0,2,4,1,3:T(2,128)S(1)}, u32[]{:S(2)}, u32[]{:S(2)}) %all-to-all-start.1) | async-done | bytes 7712 | tf_op jit(solution)/shard_map/all_to_all | solution.py:115
  110.2 4.2 %all-to-all-start.2 = ((f32[20,3,2,16,1]{0,2,4,1,3:T(2,128)}), f32[20,3,2,16,1]{0,2,4,1,3:T(2,128)S(1)}, u32[]{:S(2)}, u32[]{:S(2)}) async-start(f32[20,3,2,16,1]{0,2,4,1,3:T(2,128)} %copy.71), calls=%async_computation.2 | async-start | bytes 98304 | tf_op jit(solution)/shard_map/all_to_all | solution.py:116
  114.4 1.5 copy.67
  115.8 4.6 %all-to-all-done.2 = f32[20,3,2,16,1]{0,2,4,1,3:T(2,128)S(1)} async-done(((f32[20,3,2,16,1]{0,2,4,1,3:T(2,128)}), f32[20,3,2,16,1]{0,2,4,1,3:T(2,128)S(1)}, u32[]{:S(2)}, u32[]{:S(2)}) %all-to-all-start.2) | async-done | bytes 7712 | tf_op jit(solution)/shard_map/all_to_all | solution.py:116
  120.4 4.3 %all-to-all-start = ((f32[20,3,2,16,1,128]{5,2,1,0,4,3:T(2,128)}), f32[20,3,2,16,1,128]{5,2,1,0,4,3:T(2,128)S(1)}, u32[]{:S(2)}, u32[]{:S(2)}) async-start(f32[20,3,2,16,1,128]{5,2,1,0,4,3:T(2,128)} %copy.67), calls=%async_computation | async-start | bytes 1966080 | tf_op jit(solution)/shard_map/all_to_all | solution.py:117
  126.1 20.7 %all-to-all-done = f32[20,3,2,16,1,128]{5,2,1,0,4,3:T(2,128)S(1)} async-done(((f32[20,3,2,16,1,128]{5,2,1,0,4,3:T(2,128)}), f32[20,3,2,16,1,128]{5,2,1,0,4,3:T(2,128)S(1)}, u32[]{:S(2)}, u32[]{:S(2)}) %all-to-all-start) | async-done | bytes 983072 | tf_op jit(solution)/shard_map/all_to_all | solution.py:117
  146.8 1.2 fusion.12
  148.1 23.5 %all_gather.7 = bf16[3,2,16,2560]{3,1,0,2:T(2,128)(2,1)S(1)} all-gather(bf16[3,2,1,2560]{3,1,0,2:T(2,128)(2,1)S(1)} %copy_bitcast_fusion), channel_id=1, replica_groups=mesh['sp'=16,'hd'=2] {'sp'}, dimensions={2}, use_global_device_ids=true | all-gather | bytes 522240 | tf_op jit(solution)/shard_map/all_gather | solution.py:127
  172.3 7.0 %all-reduce.1 = bf16[3,2,16,320]{3,2,1,0:T(8,128)(2,1)S(1)} all-reduce(bf16[3,2,16,320]{3,2,1,0:T(8,128)(2,1)S(1)} %fusion.9), channel_id=2, replica_groups=mesh['sp'=16,'hd'=2] {'hd'}, use_global_device_ids=true, to_apply=%region_7.8.clone | all-reduce | flops 30720 | bytes 122880
  180.6 5.5 %all-to-all-start.3 = ((bf16[3,1,16,320]{3,0,1,2:T(4,128)(2,1)}), bf16[3,1,16,320]{3,0,1,2:T(4,128)(2,1)S(1)}, u32[]{:S(2)}, u32[]{:S(2)}) async-start(bf16[3,1,16,320]{3,0,1,2:T(4,128)(2,1)} %copy.75), calls=%async_computation.3 | async-start | bytes 98304 | tf_op jit(solution)/shard_map/all_to_all | solution.py:134
  186.1 6.0 %all-to-all-done.3 = bf16[3,1,16,320]{3,0,1,2:T(4,128)(2,1)S(1)} async-done(((bf16[3,1,16,320]{3,0,1,2:T(4,128)(2,1)}), bf16[3,1,16,320]{3,0,1,2:T(4,128)(2,1)S(1)}, u32[]{:S(2)}, u32[]{:S(2)}) %all-to-all-start.3) | async-done | bytes 30752 | tf_op jit(solution)/shard_map/all_to_all | solution.py:134
  193.3 2.6 %collective-permute-start = (bf16[5,2,1,16]{3,2,1,0:T(2,128)(2,1)S(1)}, bf16[5,2,1,16]{3,2,1,0:T(2,128)(2,1)S(1)}, u32[]{:S(2)}, u32[]{:S(2)}) collective-permute-start(bf16[5,2,1,16]{3,2,1,0:T(2,128)(2,1)S(1)} %get-tuple-element.121), channel_id=1, source_target_pairs={{0,2},{2,4},{4,6},{6,8},{8,10},{10,12},{12,14},{14,16},{16,18},{18... | collective-permute-start | bytes 968 | tf_op jit(solution)/shard_map/ppermute | solution.py:21
  196.0 1.9 collective-permute-start.1
  198.6 2.3 %collective-permute-done.1 = bf16[5,2,1,16]{3,2,1,0:T(2,128)(2,1)S(1)} collective-permute-done((bf16[5,2,1,16]{3,2,1,0:T(2,128)(2,1)S(1)}, bf16[5,2,1,16]{3,2,1,0:T(2,128)(2,1)S(1)}, u32[]{:S(2)}, u32[]{:S(2)}) %collective-permute-start.1) | collective-permute-done | bytes 352 | tf_op jit(solution)/shard_map/ppermute | solution.py:23
  201.0 2.1 %collective-permute-start.2 = (bf16[5,1,4,16]{3,2,1,0:T(4,128)(2,1)S(1)}, bf16[5,1,4,16]{3,2,1,0:T(4,128)(2,1)S(1)}, u32[]{:S(2)}, u32[]{:S(2)}) collective-permute-start(bf16[5,1,4,16]{3,2,1,0:T(4,128)(2,1)S(1)} %get-tuple-element.115), channel_id=1, source_target_pairs={{0,1},{2,3},{4,5},{6,7},{8,9},{10,11},{12,13},{14,15},{16,17},{18,... | collective-permute-start | bytes 1928 | tf_op jit(solution)/shard_map/ppermute | solution.py:21
  203.2 1.3 collective-permute-start.3
  204.6 2.9 %collective-permute-done.3 = bf16[5,1,4,16]{3,2,1,0:T(4,128)(2,1)S(1)} collective-permute-done((bf16[5,1,4,16]{3,2,1,0:T(4,128)(2,1)S(1)}, bf16[5,1,4,16]{3,2,1,0:T(4,128)(2,1)S(1)}, u32[]{:S(2)}, u32[]{:S(2)}) %collective-permute-start.3) | collective-permute-done | bytes 672 | tf_op jit(solution)/shard_map/ppermute | solution.py:23
  (216 shorter events, 64.1 us)
Async XLA Ops:
  0.6 171.0 %copy-start = (bf16[2560,320]{0,1:T(8,128)(2,1)S(1)}, bf16[2560,320]{0,1:T(8,128)(2,1)}, u32[]{:S(2)}) copy-start(bf16[2560,320]{0,1:T(8,128)(2,1)} %param.26) | copy-start | bytes 4915204
  0.6 27.7 %copy-start.9 = (s32[96]{0:T(128)S(1)}, s32[96]{0:T(128)}, u32[]{:S(2)}) copy-start(s32[96]{0:T(128)} %param.24) | copy-start | bytes 1156
  100.7 9.5 %all-to-all-start.1 = ((f32[20,3,2,16,1]{0,2,4,1,3:T(2,128)}), f32[20,3,2,16,1]{0,2,4,1,3:T(2,128)S(1)}, u32[]{:S(2)}, u32[]{:S(2)}) async-start(f32[20,3,2,16,1]{0,2,4,1,3:T(2,128)} %copy.68), calls=%async_computation.1 | async-start | bytes 98304 | tf_op jit(solution)/shard_map/all_to_all | solution.py:115
  110.2 10.2 %all-to-all-start.2 = ((f32[20,3,2,16,1]{0,2,4,1,3:T(2,128)}), f32[20,3,2,16,1]{0,2,4,1,3:T(2,128)S(1)}, u32[]{:S(2)}, u32[]{:S(2)}) async-start(f32[20,3,2,16,1]{0,2,4,1,3:T(2,128)} %copy.71), calls=%async_computation.2 | async-start | bytes 98304 | tf_op jit(solution)/shard_map/all_to_all | solution.py:116
  115.8 8.9 %copy-start.10 = (u32[32]{0:T(128)S(1)}, u32[32]{0:T(128)}, u32[]{:S(2)}) copy-start(u32[32]{0:T(128)} %constant.57) | copy-start | bytes 388
  115.8 9.5 %copy-start.4 = (f32[5120]{0:T(1024)S(1)}, f32[5120]{0:T(1024)}, u32[]{:S(2)}) copy-start(f32[5120]{0:T(1024)} %param.29) | copy-start | bytes 61444
  120.4 26.3 %all-to-all-start = ((f32[20,3,2,16,1,128]{5,2,1,0,4,3:T(2,128)}), f32[20,3,2,16,1,128]{5,2,1,0,4,3:T(2,128)S(1)}, u32[]{:S(2)}, u32[]{:S(2)}) async-start(f32[20,3,2,16,1,128]{5,2,1,0,4,3:T(2,128)} %copy.67), calls=%async_computation | async-start | bytes 1966080 | tf_op jit(solution)/shard_map/all_to_all | solution.py:117
  171.6 14.4 %copy-start.7 = (bf16[2,2,2,16]{3,2,1,0:T(2,128)(2,1)S(1)}, bf16[2,2,2,16]{3,2,1,0:T(2,128)(2,1)}, u32[]{:S(2)}) copy-start(bf16[2,2,2,16]{3,2,1,0:T(2,128)(2,1)} %param.31) | copy-start | bytes 772
  171.6 20.6 %copy-start.2 = (bf16[3,1,1,5120]{3,0,2,1:T(4,128)(2,1)S(1)}, bf16[3,1,1,5120]{3,0,2,1:T(4,128)(2,1)}, u32[]{:S(2)}) copy-start(bf16[3,1,1,5120]{3,0,2,1:T(4,128)(2,1)} %param.18) | copy-start | bytes 92164
  171.7 20.6 %copy-start.5 = (f32[5120]{0:T(1024)S(1)}, f32[5120]{0:T(1024)}, u32[]{:S(2)}) copy-start(f32[5120]{0:T(1024)} %param.27) | copy-start | bytes 61444
  171.7 21.1 %copy-start.3 = (f32[5120]{0:T(1024)S(1)}, f32[5120]{0:T(1024)}, u32[]{:S(2)}) copy-start(f32[5120]{0:T(1024)} %param.28) | copy-start | bytes 61444
  172.3 20.6 %copy-start.8 = (bf16[5120,64]{0,1:T(8,128)(2,1)S(1)}, bf16[5120,64]{0,1:T(8,128)(2,1)}, u32[]{:S(2)}) copy-start(bf16[5120,64]{0,1:T(8,128)(2,1)} %param.30) | copy-start | bytes 1966084
  180.6 11.5 %all-to-all-start.3 = ((bf16[3,1,16,320]{3,0,1,2:T(4,128)(2,1)}), bf16[3,1,16,320]{3,0,1,2:T(4,128)(2,1)S(1)}, u32[]{:S(2)}, u32[]{:S(2)}) async-start(bf16[3,1,16,320]{3,0,1,2:T(4,128)(2,1)} %copy.75), calls=%async_computation.3 | async-start | bytes 98304 | tf_op jit(solution)/shard_map/all_to_all | solution.py:134
  186.1 22.0 %copy-start.1 = (bf16[432,384]{1,0:T(8,128)(2,1)S(1)}, bf16[432,384]{1,0:T(8,128)(2,1)}, u32[]{:S(2)}) copy-start(bf16[432,384]{1,0:T(8,128)(2,1)} %param.32) | copy-start | bytes 995332
  192.5 15.9 %copy-start.6 = (f32[384]{0:T(512)S(1)}, f32[384]{0:T(512)}, u32[]{:S(2)}) copy-start(f32[384]{0:T(512)} %param.33) | copy-start | bytes 4612
  193.3 5.3 %collective-permute-start = (bf16[5,2,1,16]{3,2,1,0:T(2,128)(2,1)S(1)}, bf16[5,2,1,16]{3,2,1,0:T(2,128)(2,1)S(1)}, u32[]{:S(2)}, u32[]{:S(2)}) collective-permute-start(bf16[5,2,1,16]{3,2,1,0:T(2,128)(2,1)S(1)} %get-tuple-element.121), channel_id=1, source_target_pairs={{0,2},{2,4},{4,6},{6,8},{8,10},{10,12},{12,14},{14,16},{16,18},{18... | collective-permute-start | bytes 968 | tf_op jit(solution)/shard_map/ppermute | solution.py:21
  196.0 4.9 %collective-permute-start.1 = (bf16[5,2,1,16]{3,2,1,0:T(2,128)(2,1)S(1)}, bf16[5,2,1,16]{3,2,1,0:T(2,128)(2,1)S(1)}, u32[]{:S(2)}, u32[]{:S(2)}) collective-permute-start(bf16[5,2,1,16]{3,2,1,0:T(2,128)(2,1)S(1)} %get-tuple-element.122), channel_id=1, source_target_pairs={{2,0},{4,2},{6,4},{8,6},{10,8},{12,10},{14,12},{16,14},{18,16},{20... | collective-permute-start | bytes 968 | tf_op jit(solution)/shard_map/ppermute | solution.py:23
  201.0 3.5 %collective-permute-start.2 = (bf16[5,1,4,16]{3,2,1,0:T(4,128)(2,1)S(1)}, bf16[5,1,4,16]{3,2,1,0:T(4,128)(2,1)S(1)}, u32[]{:S(2)}, u32[]{:S(2)}) collective-permute-start(bf16[5,1,4,16]{3,2,1,0:T(4,128)(2,1)S(1)} %get-tuple-element.115), channel_id=1, source_target_pairs={{0,1},{2,3},{4,5},{6,7},{8,9},{10,11},{12,13},{14,15},{16,17},{18,... | collective-permute-start | bytes 1928 | tf_op jit(solution)/shard_map/ppermute | solution.py:21
  203.2 4.4 %collective-permute-start.3 = (bf16[5,1,4,16]{3,2,1,0:T(4,128)(2,1)S(1)}, bf16[5,1,4,16]{3,2,1,0:T(4,128)(2,1)S(1)}, u32[]{:S(2)}, u32[]{:S(2)}) collective-permute-start(bf16[5,1,4,16]{3,2,1,0:T(4,128)(2,1)S(1)} %get-tuple-element.114), channel_id=1, source_target_pairs={{1,0},{3,2},{5,4},{7,6},{9,8},{11,10},{13,12},{15,14},{17,16},{19,... | collective-permute-start | bytes 1928 | tf_op jit(solution)/shard_map/ppermute | solution.py:23
where the time goes:
time: 212 us; the launch traced here: 209 us
  blocking collectives  55 us (26%)
  waiting for transfers between devices  41.7 us (20%)
  matrix products  40.2 us (19%)
  starting transfers between devices  25.3 us (12%)
  local copies, waits for them, and re-layouts  23.6 us (11%)
  loops' own time  13.6 us (6%)
  other arithmetic  7.96 us (4%)
    all_gather x1, blocking collectives, local(): gathered = lax.all_gather(queries, 'sp', axis=2, tiled=True)  24.6 us
    all_gather x1, blocking collectives, local(): lax.all_gather(attended, 'sp', axis=2, tiled=True)  23.5 us
    all_to_all x1, waiting for transfers between devices, local(): lax.all_to_all(out_parts, 'sp', split_axis=3, concat_axis=4, tiled=True)  20.7 us
    dot_general x20, matrix products, head_partials(): lax.dot_general(query_part, key_part, (((1,), (1,)), ((), ())), preferred...  19.9 us
    dot_general x20, matrix products, head_partials(): summed = jnp.dot(weights, value_part, preferred_element_type=jnp.float32)  19.1 us
    another operation x1, loops' own time, local(): lax.map(one_head, jnp.arange(head_count, dtype=jnp.int32))  13.6 us
    dynamic_slice x20, local copies, waits for them, and re-layouts, local(): lax.map(one_head, jnp.arange(head_count, dtype=jnp.int32))  11.7 us
    unnamed x1, blocking collectives  6.96 us
  transfers between devices with their start and end apart: 8, of which 6 were waited for; matrix products, arithmetic and copies ran while one was open for 2% of the time, Pallas kernels for 0%

commit v1 on v0

v1 whole, which is shorter than its diff:
```python
import functools
import math

import jax
import jax.numpy as jnp
import numpy as np
from jax import lax
from jax.experimental import pallas as pl
from jax.experimental.pallas import tpu as pltpu
from jax.sharding import PartitionSpec as P

HDIM = 128
LANES = 128
MESH = pl.DeviceIdType.MESH
F32 = jnp.float32
BF16 = jnp.bfloat16


def up(value, unit):
    return -(-value // unit) * unit


class Sizes:
    def __init__(self, mesh, queries, cache_k, out_weight):
        self.nsp, self.nhd = mesh.shape["sp"], mesh.shape["hd"]
        self.nchip = self.nsp // 2
        self.frames, self.rows, _, self.width = queries.shape
        self.heads = self.width // HDIM
        self.own = self.rows // self.nhd
        self.tokens = self.frames * self.rows
        self.slot = up(self.own * self.frames, 4)
        self.tp = self.slot * self.nhd
        self.halves = 2 if self.tp % 16 and self.heads % 2 == 0 else 1
        if self.halves == 1:
            self.tp = up(self.tp, 16)
        self.block = self.halves * self.tp
        self.lanes = self.width // self.halves
        self.pairs = self.heads // self.halves
        self.cache = cache_k.shape[0]
        self.span = up(self.tp, 16)
        self.keys = self.cache + self.span
        self.all = self.nsp * self.block
        self.part = out_weight.shape[1]
        self.pieces = -(-self.part // LANES)
        self.message = up(self.pieces * self.slot, 16)
        self.model = self.part * self.nsp

    def slots(self):
        for f in range(self.frames):
            for r in range(self.rows):
                yield (r // self.own) * self.slot + (r % self.own) * self.frames + f, f, r


def iota(shape, dim):
    return lax.broadcasted_iota(jnp.int32, shape, dim)


def merge_stats(stats):
    top = functools.reduce(jnp.maximum, stats)
    scales = [jnp.exp(s - top) for s in stats]
    total = functools.reduce(
        jnp.add, [s * pltpu.roll(a, 64, 1) for s, a in zip(stats, scales)]
    )
    return top, total, scales


def kernel(
    z, q_ref, k_ref, v_ref, valid_ref, stream_ref, gate_ref, shift_ref, scale_ref, latc_ref, gain_ref,
    ck_hbm, cv_hbm, w_hbm, hw_hbm, cw_hbm,
    so_ref, dec_ref,
    g, att, o, st, o_in, s_in, co, cs, o_got, s_got, k2, v2, w, hw, cw, zs, z_got, h, r_got, near, msg, tmp,
    local_sem, ag_send, ag_recv, fw_send, fw_recv, sib_send, sib_recv, b_send, b_recv,
    hd_send, hd_recv, e_send, e_recv, n_send, n_recv,
):
    me, my = lax.axis_index("sp"), lax.axis_index("hd")
    core, chip = me % 2, me // 2
    sib = me + 1 - 2 * core
    nchip, block = z.nchip, z.block

    def peer(k):
        return (chip + k) % nchip

    def source(k):
        return (chip + nchip - k) % nchip

    def rows_of(which_core, which_chip):
        return pl.ds(pl.multiple_of((which_core * nchip + which_chip) * block, block), block)

    def chip_rows(which_chip):
        return pl.ds(pl.multiple_of(which_chip * block, block), block)

    def remote(src, dst, ssem, rsem, sp, hd):
        return pltpu.make_async_remote_copy(
            src_ref=src, dst_ref=dst, send_sem=ssem, recv_sem=rsem,
            device_id=(sp, hd), device_id_type=MESH,
        )

    loads = []

    def load(src, dst):
        copy = pltpu.make_async_copy(src, dst, local_sem.at[len(loads)])
        copy.start()
        loads.append(copy)

    for half in range(z.halves):
        cols = pl.ds(half * z.lanes, z.lanes)
        load(ck_hbm.at[:, cols], k2.at[pl.ds(half * z.keys, z.cache)])
        load(cv_hbm.at[:, cols], v2.at[pl.ds(half * z.keys, z.cache)])
    attention_loads = len(loads)
    load(w_hbm, w)
    load(hw_hbm, hw)
    load(cw_hbm, cw)

    def packed(ref):
        row = iota((z.tp, z.width), 0)
        out = jnp.zeros((z.tp, z.width), F32)
        for slot, f, r in z.slots():
            out = jnp.where(row == slot, ref[f, r].astype(F32), out)
        return [out[:, i * z.lanes : (i + 1) * z.lanes] for i in range(z.halves)]

    g[rows_of(core, chip), :] = jnp.concatenate(packed(q_ref), axis=0).astype(BF16)
    near[...] = jnp.zeros_like(near)

    barrier = pltpu.get_barrier_semaphore()
    for k in range(1, z.nsp):
        pl.semaphore_signal(barrier, inc=1, device_id=((me + k) % z.nsp, my), device_id_type=MESH)
    for k in range(1, z.nhd):
        pl.semaphore_signal(barrier, inc=1, device_id=(me, (my + k) % z.nhd), device_id_type=MESH)

    def inside(dr, dc):
        ok = None
        for step, at, count in ((dr, my, z.nhd), (dc, me, z.nsp)):
            if step:
                here = (at + step >= 0) & (at + step < count)
                ok = here if ok is None else ok & here
        return ok

    greeted = z.nsp - 1 + z.nhd - 1
    for dr in (-1, 1):
        for dc in (-1, 1):

            @pl.when(inside(dr, dc))
            def _():
                pl.semaphore_signal(barrier, inc=1, device_id=(me + dc, my + dr), device_id_type=MESH)

            greeted = greeted + inside(dr, dc).astype(jnp.int32)
    pl.semaphore_wait(barrier, greeted)

    def gather_start(buf, phase):
        mine = rows_of(core, chip)
        first = [
            remote(buf.at[mine], buf.at[mine], ag_send.at[phase, k], ag_recv.at[phase, k],
                   peer(k) * 2 + core, my)
            for k in range(1, nchip)
        ]
        for copy in first:
            copy.start()
        return first

    def gather_finish(buf, phase, first):
        forwards = []
        for k in range(nchip):
            if k:
                first[k - 1].wait_recv()
            rows = rows_of(core, source(k))
            copy = remote(buf.at[rows], buf.at[rows], fw_send.at[phase, k], fw_recv.at[phase, k], sib, my)
            copy.start()
            forwards.append(copy)
        for copy in forwards:
            copy.wait_recv()
        return first + forwards

    first = gather_start(g, 0)
    for ref, buf in ((k_ref, k2), (v_ref, v2)):
        for half, part in enumerate(packed(ref)):
            if z.span > z.tp:
                part = jnp.concatenate([part, jnp.zeros((z.span - z.tp, z.lanes), F32)], axis=0)
            buf[pl.ds(half * z.keys + z.cache, z.span), :] = part.astype(BF16)
    for copy in loads[:attention_loads]:
        copy.wait()
    sent = gather_finish(g, 0, first)

    chunk = min(z.all, 256)
    total_keys = z.halves * z.keys
    lane = iota((chunk, LANES), 1)
    scale = 1.0 / math.sqrt(HDIM)
    mask = valid_ref[...] > 0.0
    if z.halves > 1:
        row_half = (iota((chunk, total_keys), 0) // z.tp) % z.halves
        col_half = (iota((chunk, total_keys), 1) >= z.keys).astype(jnp.int32)
        mask = mask & (row_half == col_half)
    else:
        mask = jnp.broadcast_to(mask, (chunk, total_keys))

    def attend(at, carry):
        rows = pl.ds(pl.multiple_of(at * chunk, chunk), chunk)
        stats = jnp.zeros((chunk, LANES), F32)
        for j in range(z.pairs):
            cols = pl.ds(j * HDIM, HDIM)
            scores = lax.dot_general(
                g[rows, cols], k2[:, cols], (((1,), (1,)), ((), ())), preferred_element_type=F32
            )
            scores = jnp.where(mask, scores * scale, -1e30)
            top = jnp.max(scores, axis=1, keepdims=True)
            weights = jnp.exp(scores - top).astype(BF16)
            total = jnp.sum(weights.astype(F32), axis=1, keepdims=True)
            out = jnp.dot(weights, v2[:, cols], preferred_element_type=F32)
            o[rows, cols] = out.astype(BF16)
            stats = jnp.where(lane == j, top, jnp.where(lane == j + 64, total, stats))
        st[rows, :] = stats
        return carry

    lax.fori_loop(0, z.all // chunk, attend, 0)

    half_rows = nchip * block
    theirs = pl.ds(pl.multiple_of((1 - core) * half_rows, half_rows), half_rows)
    pair = [
        remote(st.at[theirs], s_in, sib_send.at[0], sib_recv.at[0], sib, my),
        remote(o.at[theirs], o_in, sib_send.at[1], sib_recv.at[1], sib, my),
    ]
    for copy in pair:
        copy.start()
    for copy in sent:
        copy.wait_send()
    for copy in pair:
        copy.wait_recv()

    low = iota((block, LANES), 1) < 64
    exchanged = []
    for k in list(range(1, nchip)) + [0]:
        to = peer(k)
        mine, rows = rows_of(core, to), chip_rows(to)
        top, total, (a, b) = merge_stats([st[mine, :], s_in[rows, :]])
        cs[rows, :] = jnp.where(low, top, total)
        for j in range(z.pairs):
            cols = pl.ds(j * HDIM, HDIM)
            merged = (
                o[mine, cols].astype(F32) * a[:, j : j + 1]
                + o_in[rows, cols].astype(F32) * b[:, j : j + 1]
            )
            co[rows, cols] = merged.astype(BF16)
        if k:
            there = chip_rows(chip)
            for which, (src, dst) in enumerate(((cs, s_got), (co, o_got))):
                copy = remote(src.at[rows], dst.at[there], b_send.at[which, k], b_recv.at[which, k],
                              to * 2 + core, my)
                copy.start()
                exchanged.append(copy)
    own_rows = chip_rows(chip)
    s_got[own_rows, :] = cs[own_rows, :]
    o_got[own_rows, :] = co[own_rows, :]
    for copy in exchanged:
        copy.wait_recv()

    top, total, scales = merge_stats([s_got[pl.ds(i * block, block), :] for i in range(nchip)])
    inverse = pltpu.roll(1.0 / jnp.where(low, 1.0, total), 64, 1)
    for j in range(z.pairs):
        cols = pl.ds(j * HDIM, HDIM)
        summed = functools.reduce(
            jnp.add,
            [
                o_got[pl.ds(i * block, block), cols].astype(F32) * scales[i][:, j : j + 1]
                for i in range(nchip)
            ],
        )
        att[rows_of(core, chip), cols] = (summed * inverse[:, j : j + 1]).astype(BF16)

    first = gather_start(att, 1)
    for copy in pair + exchanged:
        copy.wait_send()
    for copy in loads[attention_loads:]:
        copy.wait()
    sent = gather_finish(att, 1, first)

    everything = att[...]
    proj = None
    for half in range(z.halves):
        term = jnp.dot(everything, w[pl.ds(half * z.lanes, z.lanes), :], preferred_element_type=F32)
        term = term.reshape(z.nsp, z.halves, z.tp, z.part)[:, half]
        proj = term if proj is None else proj + term
    proj = proj.reshape(z.nsp * z.tp, z.part).astype(BF16)
    out_rows, in_rows = z.nsp * z.message, z.nsp * z.tp
    out_at, in_at = iota((out_rows, in_rows), 0), iota((out_rows, in_rows), 1)
    out_sp, inner = out_at // z.message, out_at % z.message
    base = ((out_sp % 2) * nchip + out_sp // 2) * z.tp + inner % z.slot
    for owner in range(z.nhd):
        wanted = in_at == base + owner * z.slot
        cells = []
        moved = jnp.zeros((out_rows, LANES), F32)
        for piece in range(z.pieces):
            wide = min(LANES, z.part - piece * LANES)
            pick = jnp.where(wanted & (inner // z.slot == piece), 1.0, 0.0).astype(BF16)
            got = jnp.dot(pick, proj[:, piece * LANES : piece * LANES + wide], preferred_element_type=F32)
            if wide < LANES:
                got = jnp.concatenate([got, jnp.zeros((out_rows, LANES - wide), F32)], axis=1)
            moved = moved + got
        zs[owner] = moved.astype(BF16)

    swaps = []
    for k in range(1, z.nhd):
        to = (my + k) % z.nhd
        copy = remote(zs.at[to], z_got.at[my], hd_send.at[k], hd_recv.at[k], me, to)
        copy.start()
        swaps.append(copy)
    for copy in sent:
        copy.wait_send()
    summed = zs[my].astype(F32)
    for k in range(1, z.nhd):
        swaps[k - 1].wait_recv()
        summed = summed + z_got[(my + z.nhd - k) % z.nhd].astype(F32)
    h[...] = summed.astype(BF16)

    def message_rows(at):
        return pl.ds(pl.multiple_of(at * z.message, z.message), z.message)

    spread = []
    for k in range(1, z.nsp):
        to = (me + k) % z.nsp
        copy = remote(h.at[message_rows(to)], r_got.at[message_rows(me)], e_send.at[k], e_recv.at[k], to, my)
        copy.start()
        spread.append(copy)
    r_got[message_rows(me), :] = h[message_rows(me), :]
    for copy in swaps:
        copy.wait_send()
    for copy in spread:
        copy.wait_recv()

    got_all = r_got[...]
    to_rows, from_rows = z.nsp * 8, z.nsp * z.message
    to_at, from_at = iota((to_rows, from_rows), 0), iota((to_rows, from_rows), 1)
    by_piece = []
    for piece in range(z.pieces):
        pick = (from_at == (to_at // 8) * z.message + piece * z.slot + to_at % 8) & (to_at % 8 < z.slot)
        by_piece.append(jnp.dot(jnp.where(pick, 1.0, 0.0).astype(BF16), got_all, preferred_element_type=F32))
    lane8 = iota((8, LANES), 1)
    row8 = iota((8, LANES), 0)
    tiles = []
    for tile in range(z.model // LANES):
        value = jnp.zeros((8, LANES), F32)
        begin = tile * LANES
        for s in range(begin // z.part, (begin + LANES - 1) // z.part + 1):
            for piece in range(z.pieces):
                low_at = s * z.part + piece * LANES
                high_at = min(low_at + LANES, (s + 1) * z.part)
                a, b = max(low_at, begin), min(high_at, begin + LANES)
                if a >= b:
                    continue
                cell = by_piece[piece][s * 8 : (s + 1) * 8]
                if (low_at - begin) % LANES:
                    cell = pltpu.roll(cell, (low_at - begin) % LANES, 1)
                value = jnp.where((lane8 >= a - begin) & (lane8 < b - begin), cell, value)
        cols = pl.ds(begin, LANES)
        base_value = jnp.zeros((8, LANES), F32)
        for f in range(z.frames):
            base_value = jnp.where(row8 == f, stream_ref[f, :, cols].astype(F32), base_value)
        value = base_value + gate_ref[:, cols] * value
        value = value.astype(BF16).astype(F32)
        so_ref[:, cols] = value
        tiles.append(value)
    mean = jnp.sum(functools.reduce(jnp.add, tiles), axis=1, keepdims=True) / z.model
    centred = [t - mean for t in tiles]
    variance = jnp.sum(functools.reduce(jnp.add, [t * t for t in centred]), axis=1, keepdims=True) / z.model
    root = lax.rsqrt(variance + 1e-6)
    normed = []
    for tile, t in enumerate(centred):
        cols = pl.ds(tile * LANES, LANES)
        normed.append(t * root * (1.0 + scale_ref[:, cols]) + shift_ref[:, cols])
    normed = jnp.concatenate(normed, axis=1)
    normed = jnp.concatenate([normed, jnp.zeros_like(normed)], axis=0).astype(BF16)
    patch = jnp.dot(normed, hw[...], preferred_element_type=F32)
    cells = patch.shape[1]
    past = latc_ref.shape[0]
    tmp[...] = jnp.zeros_like(tmp)
    tmp[0:past, 0:cells] = latc_ref[...]
    tmp[past : past + z.frames, 0:cells] = patch[0 : z.frames]
    msg[...] = tmp[...].astype(BF16)

    order = [(dr, dc) for dr in (-1, 0, 1) for dc in (-1, 0, 1) if (dr, dc) != (0, 0)]

    def halo(dr, dc):
        at = (dr + 1) * 3 + dc + 1
        return remote(msg, near.at[8 - at], n_send.at[at], n_recv.at[8 - at], me + dc, my + dr)

    for dr, dc in order:

        @pl.when(inside(dr, dc))
        def _():
            halo(dr, dc).start()

    near[4] = msg[...]
    for copy in spread:
        copy.wait_send()
    for dr, dc in order:

        @pl.when(inside(dr, dc))
        def _():
            copy = halo(dr, dc)
            copy.wait_send()
            pltpu.make_async_remote_copy(
                src_ref=msg, dst_ref=near.at[(dr + 1) * 3 + dc + 1],
                send_sem=n_send.at[(dr + 1) * 3 + dc + 1], recv_sem=n_recv.at[(dr + 1) * 3 + dc + 1],
                device_id=(me + dc, my + dr), device_id_type=MESH,
            ).wait_recv()

    around = [near[i].astype(F32)[0:8] for i in range(9)]
    chan = cells // 4
    taps = 9 * chan
    wide_taps, rest_taps = [], []
    for i in range(2):
        for j in range(2):
            parts = [jnp.zeros((8, LANES), F32), jnp.zeros((8, LANES), F32)]
            for v in range(3):
                for u in range(3):
                    ri, ci = i + v - 1, j + u - 1
                    at = (ri // 2 + 1) * 3 + ci // 2 + 1
                    src = ((ri % 2) * 2 + ci % 2) * chan
                    to = (v * 3 + u) * chan
                    shift = (to - src) % LANES
                    cell = pltpu.roll(around[at], shift, 1) if shift else around[at]
                    inner_at = to % LANES
                    parts[to // LANES] = jnp.where(
                        (lane8 >= inner_at) & (lane8 < inner_at + chan), cell, parts[to // LANES]
                    )
            wide_taps.append(parts[0])
            rest_taps.append(parts[1])
    wide_taps = jnp.concatenate(wide_taps, axis=0).astype(BF16)
    rest_taps = jnp.concatenate(rest_taps, axis=0).astype(BF16)[:, : taps - LANES]
    steps = []
    for u in range(3):
        steps.append(
            jnp.dot(wide_taps, cw[pl.ds(u * taps, LANES), :], preferred_element_type=F32)
            + jnp.dot(rest_taps, cw[pl.ds(u * taps + LANES, taps - LANES), :], preferred_element_type=F32)
        )
    for cell in range(4):
        rows = slice(cell * 8, cell * 8 + 8)
        conv = steps[0][rows] + pltpu.roll(steps[1][rows], 7, 0) + pltpu.roll(steps[2][rows], 6, 0)
        square = jnp.sum(conv * conv, axis=1, keepdims=True) / conv.shape[1]
        scaled = conv * lax.rsqrt(square + 1e-6) * gain_ref[...]
        dec_ref[cell] = scaled / (1.0 + jnp.exp(-scaled))


def local(
    mesh, stream, queries, span_k, span_v, cache_k, cache_v, cache_age, history, out_weight,
    attn_gate, head_shift, head_scale, head_weight, latent_cache, conv_weight, rms_gain,
):
    z = Sizes(mesh, queries, cache_k, out_weight)
    span_valid = np.zeros((z.span,), np.float32)
    for slot, _, _ in z.slots():
        span_valid[slot] = 1.0
    valid = jnp.concatenate([jnp.where(cache_age < history[0], 1.0, 0.0).astype(F32), jnp.asarray(span_valid)])
    valid = jnp.tile(valid, z.halves)[None, :]
    model, chan = z.model, conv_weight.shape[1]
    past = latent_cache.shape[0]
    latc = latent_cache.reshape(past, -1).astype(F32)
    vmem = pl.BlockSpec(memory_space=pltpu.VMEM)
    hbm = pl.BlockSpec(memory_space=pl.ANY)
    half = z.all // 2
    dma = lambda *shape: pltpu.SemaphoreType.DMA(shape)
    out, dec = pl.pallas_call(
        functools.partial(kernel, z),
        out_shape=(jax.ShapeDtypeStruct((8, model), F32), jax.ShapeDtypeStruct((4, 8, chan), F32)),
        in_specs=[vmem] * 10 + [hbm] * 5,
        out_specs=(vmem, vmem),
        scratch_shapes=[
            pltpu.VMEM((z.all, z.lanes), BF16),
            pltpu.VMEM((z.all, z.lanes), BF16),
            pltpu.VMEM((z.all, z.lanes), BF16),
            pltpu.VMEM((z.all, LANES), F32),
            pltpu.VMEM((half, z.lanes), BF16),
            pltpu.VMEM((half, LANES), F32),
            pltpu.VMEM((half, z.lanes), BF16),
            pltpu.VMEM((half, LANES), F32),
            pltpu.VMEM((half, z.lanes), BF16),
            pltpu.VMEM((half, LANES), F32),
            pltpu.VMEM((z.halves * z.keys, z.lanes), BF16),
            pltpu.VMEM((z.halves * z.keys, z.lanes), BF16),
            pltpu.VMEM(out_weight.shape, BF16),
            pltpu.VMEM(head_weight.shape, BF16),
            pltpu.VMEM(conv_weight.shape, BF16),
            pltpu.VMEM((z.nhd, z.nsp * z.message, LANES), BF16),
            pltpu.VMEM((z.nhd, z.nsp * z.message, LANES), BF16),
            pltpu.VMEM((z.nsp * z.message, LANES), BF16),
            pltpu.VMEM((z.nsp * z.message, LANES), BF16),
            pltpu.VMEM((9, 16, LANES), BF16),
            pltpu.VMEM((16, LANES), BF16),
            pltpu.VMEM((16, LANES), F32),
            dma(2 * z.halves + 3),
            dma(2, z.nchip), dma(2, z.nchip), dma(2, z.nchip), dma(2, z.nchip),
            dma(2), dma(2),
            dma(2, z.nchip), dma(2, z.nchip),
            dma(z.nhd), dma(z.nhd),
            dma(z.nsp), dma(z.nsp),
            dma(9), dma(9),
        ],
        compiler_params=pltpu.CompilerParams(
            collective_id=0, has_side_effects=True, vmem_limit_bytes=56 * 1024 * 1024
        ),
        name="span_block",
    )(
        queries, span_k, span_v, valid, stream.reshape(z.frames, 1, model),
        attn_gate[None], head_shift[None], head_scale[None], latc, rms_gain[None],
        cache_k, cache_v, out_weight, head_weight, conv_weight,
    )
    stream_out = out[: z.frames].astype(BF16).reshape(stream.shape)
    decoded = jnp.transpose(dec.reshape(2, 2, 8, chan)[:, :, : z.frames], (2, 0, 1, 3)).astype(BF16)
    return stream_out, decoded


def solution(mesh):
    placed = (
        P(None, "hd", "sp", None),
        P(None, None, "sp", "hd"),
        P(None, None, "sp", "hd"),
        P(None, None, "sp", "hd"),
        P("sp", "hd"),
        P("sp", "hd"),
        P("sp"),
        P(),
        P("hd", "sp"),
        P(),
        P(),
        P(),
        P(),
        P(None, "hd", "sp", None),
        P(),
        P(),
    )
    return jax.shard_map(
        functools.partial(local, mesh),
        mesh=mesh,
        in_specs=placed,
        out_specs=(P(None, "hd", "sp", None), P(None, "hd", "sp", None)),
        check_vma=False,
    )
```

time: 212 us -> 73.7 us (0.35)
  blocking collectives: 55 us -> 0 us
  Pallas kernels: 0 us -> 53.3 us
  waiting for transfers between devices: 41.7 us -> 0 us
  matrix products: 40.2 us -> 0 us
  starting transfers between devices: 25.3 us -> 0 us
  loops' own time: 13.6 us -> 0 us
  local copies, waits for them, and re-layouts: 23.6 us -> 15.8 us
  other arithmetic: 7.96 us -> 2.19 us
    pallas_call x0 -> x1, Pallas kernels: none -> 53.3 us  [local(): pl.pallas_call(functools.partial(kernel, z), out_shape=(jax.ShapeDtypeStr...]
    all_gather x2 -> x0, blocking collectives: 48.1 us -> none  [the longest x1 24.6 us: local(): gathered = lax.all_gather(queries, 'sp', axis=2, tiled=True)]
    dot_general x43 -> x0, matrix products: 40.2 us -> none  [the longest x20 19.9 us: head_partials(): lax.dot_general(query_part, key_part, (((1,), (1,)), ((), ())), preferred...]
    all_to_all x4 -> x0, waiting for transfers between devices: 36.5 us -> none  [the longest x1 20.7 us: local(): lax.all_to_all(out_parts, 'sp', split_axis=3, concat_axis=4, tiled=True)]
    all_to_all x4 -> x0, starting transfers between devices: 17.4 us -> none  [the longest x1 5.45 us: local(): lax.all_to_all(head_terms.astype(jnp.bfloat16), 'sp', split_axis=2, conca...]
    another operation x1 -> x0, loops' own time: 13.6 us -> none  [local(): lax.map(one_head, jnp.arange(head_count, dtype=jnp.int32))]
    dynamic_slice x20 -> x0, local copies, waits for them, and re-layouts: 11.7 us -> none  [local(): lax.map(one_head, jnp.arange(head_count, dtype=jnp.int32))]
    ppermute x4 -> x0, starting transfers between devices: 7.96 us -> none  [the longest x2 4.75 us: padded_2(): lax.ppermute(tail, axis, [(i, (i + 1) % count) for i in range(ends)])]
  transfers between devices with their start and end apart: 8 -> 0, of which waited for: 6 -> 0; matrix products, arithmetic and copies ran while one was open for 2% -> 0% of each run, Pallas kernels for 0% -> 0%
where the time goes in v1:
time: 73.7 us; the launch traced here: 72.7 us
  Pallas kernels  53.3 us (72%)
  local copies, waits for them, and re-layouts  15.8 us (21%)
  other arithmetic  2.19 us (3%)
  between operations  1.42 us (2%)
    pallas_call x1, Pallas kernels, local(): pl.pallas_call(functools.partial(kernel, z), out_shape=(jax.ShapeDtypeStr...  53.3 us
    unnamed x8, local copies, waits for them, and re-layouts  9.57 us
    reshape x1, local copies, waits for them, and re-layouts, local(): stream_out = out[:z.frames].astype(BF16).reshape(stream.shape)  1.55 us

profile of v1, /device:TPU:1, one launch (start us, length us, event | category | flops | bytes accessed | tf_op | source)
XLA Modules:
  0.0 72.7 jit_solution(14020093801414347045)
XLA Ops:
  0.6 0.0 copy-start
  1.4 0.7 compare_select_fusion
  2.1 0.7 %pad_maximum_fusion = f32[112]{0:T(128)S(1)} fusion(f32[16]{0:T(128)} %constant.6.clone, f32[96]{0:T(128)S(1)} %compare_select_fusion), kind=kLoop, calls=%fused_computation.4 | loop fusion | flops 112 | bytes 896 | tf_op jit(solution)/shard_map/concatenate | solution.py:450
  2.8 0.6 broadcast_in_dim_tile.3.valid_ref
  3.4 1.3 %reshape.21.latc_ref = f32[2,64]{1,0:T(2,128)} reshape(bf16[2,2,2,16]{3,2,1,0:T(2,128)(2,1)} %param.30) | data formatting | bytes 768 | tf_op jit(solution)/shard_map/convert_element_type | solution.py:454
  4.7 1.2 %broadcast_in_dim.25.gain_ref = f32[1,384]{1,0:T(1,128)} reshape(f32[384]{0:T(512)} %param.32) | data formatting | bytes 3072 | tf_op jit(solution)/shard_map/broadcast_in_dim | solution.py:501
  6.0 1.4 %copy.28.stream_ref = bf16[3,1,5120]{2,1,0:T(2,128)(2,1)} copy(bf16[3,1,5120]{2,0,1:T(4,128)(2,1)} %bitcast.13) | data formatting | bytes 61440 | tf_op jit(solution)/shard_map/reshape | solution.py:500
  7.4 1.4 %copy.25.q_ref = bf16[3,2,1,2560]{3,2,1,0:T(2,128)(2,1)} copy(bf16[3,2,1,2560]{3,1,2,0:T(2,128)(2,1)} %param.18) | data formatting | bytes 61440 | tf_op args[1]
  8.9 1.4 %copy.26.k_ref = bf16[3,2,1,2560]{3,2,1,0:T(2,128)(2,1)} copy(bf16[3,2,1,2560]{3,1,2,0:T(2,128)(2,1)} %param.19) | data formatting | bytes 61440 | tf_op args[2]
  10.3 1.4 %copy.27.v_ref = bf16[3,2,1,2560]{3,2,1,0:T(2,128)(2,1)} copy(bf16[3,2,1,2560]{3,1,2,0:T(2,128)(2,1)} %param.20) | data formatting | bytes 61440 | tf_op args[3]
  11.7 2.3 %copy.30.hw_hbm = bf16[5120,64]{1,0:T(8,128)(2,1)} copy(bf16[5120,64]{0,1:T(8,128)(2,1)} %param.29) | data formatting | bytes 1310720 | tf_op args[12]
  14.0 0.0 copy-done
  14.0 2.4 %copy.29.w_hbm = bf16[2560,320]{1,0:T(8,128)(2,1)} copy(bf16[2560,320]{0,1:T(8,128)(2,1)S(1)} %copy-done) | data formatting | bytes 3276800 | tf_op args[8]
  16.4 53.3 %span_block.1 = (f32[8,5120]{1,0:T(8,128)}, f32[4,8,384]{2,1,0:T(8,128)}) custom-call(bf16[3,2,1,2560]{3,2,1,0:T(2,128)(2,1)} %copy.25.q_ref, bf16[3,2,1,2560]{3,2,1,0:T(2,128)(2,1)} %copy.26.k_ref, bf16[3,2,1,2560]{3,2,1,0:T(2,128)(2,1)} %copy.27.v_ref, f32[1,224]{1,0:T(1,128)} %broadcast_in_dim_tile.3.valid_ref, bf16[3,1,5120]{2,1,0:T(2,128)(2,1)} %copy.28.stream_ref, ...), custom_call_target="tpu_custom_call" | custom-call | tf_op jit(solution)/shard_map/span_block/pallas_call | solution.py:459
  69.7 1.5 %fusion = bf16[3,1,1,5120]{3,0,2,1:T(4,128)(2,1)} fusion(f32[8,5120]{1,0:T(8,128)} %get-tuple-element.4), kind=kLoop, calls=%fused_computation.1 | loop fusion | bytes 61440 | tf_op jit(solution)/shard_map/reshape | solution.py:504
  71.3 0.8 %convert.9 = bf16[4,8,384]{2,1,0:T(8,128)(2,1)S(1)} convert(f32[4,8,384]{2,1,0:T(8,128)} %get-tuple-element.5) | non-fusion elementwise | flops 12288 | bytes 73728 | tf_op jit(solution)/shard_map/convert.2
  72.1 0.6 copy.34
  (2 shorter events, 0.0 us)
Async XLA Ops:
  0.6 13.4 %copy-start = (bf16[2560,320]{0,1:T(8,128)(2,1)S(1)}, bf16[2560,320]{0,1:T(8,128)(2,1)}, u32[]{:S(2)}) copy-start(bf16[2560,320]{0,1:T(8,128)(2,1)} %param.25) | copy-start | bytes 4915204

commit v2 on v1

--- a/solution.py
+++ b/solution.py
@@ -3,7 +3,6 @@
 
 import jax
 import jax.numpy as jnp
-import numpy as np
 from jax import lax
 from jax.experimental import pallas as pl
 from jax.experimental.pallas import tpu as pltpu
@@ -24,7 +23,7 @@
     def __init__(self, mesh, queries, cache_k, out_weight):
         self.nsp, self.nhd = mesh.shape["sp"], mesh.shape["hd"]
         self.nchip = self.nsp // 2
-        self.frames, self.rows, _, self.width = queries.shape
+        self.frames, self.rows, self.width = queries.shape
         self.heads = self.width // HDIM
         self.own = self.rows // self.nhd
         self.tokens = self.frames * self.rows
@@ -37,10 +36,10 @@
         self.lanes = self.width // self.halves
         self.pairs = self.heads // self.halves
         self.cache = cache_k.shape[0]
-        self.span = up(self.tp, 16)
-        self.keys = self.cache + self.span
+        self.keys = up(self.cache + up(self.tp, 16), LANES)
+        self.span = self.keys - self.cache
         self.all = self.nsp * self.block
-        self.part = out_weight.shape[1]
+        self.part = out_weight.shape[0]
         self.pieces = -(-self.part // LANES)
         self.message = up(self.pieces * self.slot, 16)
         self.model = self.part * self.nsp
@@ -65,10 +64,10 @@
 
 
 def kernel(
-    z, q_ref, k_ref, v_ref, valid_ref, stream_ref, gate_ref, shift_ref, scale_ref, latc_ref, gain_ref,
+    z, q_ref, k_ref, v_ref, age_ref, history_ref, stream_ref, gate_ref, shift_ref, scale_ref, latc_ref, gain_ref,
     ck_hbm, cv_hbm, w_hbm, hw_hbm, cw_hbm,
     so_ref, dec_ref,
-    g, att, o, st, o_in, s_in, co, cs, o_got, s_got, k2, v2, w, hw, cw, zs, z_got, h, r_got, near, msg, tmp,
+    g, att, o, st, o_in, s_in, co, cs, o_got, s_got, k2, v2, w, hw, cw, zs, z_got, h, r_got, near, msg, tmp, pick_out, pick_in,
     local_sem, ag_send, ag_recv, fw_send, fw_recv, sib_send, sib_recv, b_send, b_recv,
     hd_send, hd_recv, e_send, e_recv, n_send, n_recv,
 ):
@@ -95,6 +94,38 @@
             device_id=(sp, hd), device_id_type=MESH,
         )
 
+    def packed(ref):
+        row = iota((z.tp, z.width), 0)
+        out = jnp.zeros((z.tp, z.width), F32)
+        for slot, f, r in z.slots():
+            out = jnp.where(row == slot, ref[f, r : r + 1, :].astype(F32), out)
+        return [out[:, i * z.lanes : (i + 1) * z.lanes] for i in range(z.halves)]
+
+    near[...] = jnp.zeros_like(near)
+
+    barrier = pltpu.get_barrier_semaphore()
+    for k in range(1, z.nsp):
+        pl.semaphore_signal(barrier, inc=1, device_id=((me + k) % z.nsp, my), device_id_type=MESH)
+    for k in range(1, z.nhd):
+        pl.semaphore_signal(barrier, inc=1, device_id=(me, (my + k) % z.nhd), device_id_type=MESH)
+
+    def inside(dr, dc):
+        ok = None
+        for step, at, count in ((dr, my, z.nhd), (dc, me, z.nsp)):
+            if step:
+                here = (at + step >= 0) & (at + step < count)
+                ok = here if ok is None else ok & here
+        return ok
+
+    greeted = z.nsp - 1 + z.nhd - 1
+    for dr in (-1, 1):
+        for dc in (-1, 1):
+
+            @pl.when(inside(dr, dc))
+            def _():
+                pl.semaphore_signal(barrier, inc=1, device_id=(me + dc, my + dr), device_id_type=MESH)
+
+            greeted = greeted + inside(dr, dc).astype(jnp.int32)
     loads = []
 
     def load(src, dst):
@@ -111,39 +142,7 @@
     load(hw_hbm, hw)
     load(cw_hbm, cw)
 
-    def packed(ref):
-        row = iota((z.tp, z.width), 0)
-        out = jnp.zeros((z.tp, z.width), F32)
-        for slot, f, r in z.slots():
-            out = jnp.where(row == slot, ref[f, r].astype(F32), out)
-        return [out[:, i * z.lanes : (i + 1) * z.lanes] for i in range(z.halves)]
-
     g[rows_of(core, chip), :] = jnp.concatenate(packed(q_ref), axis=0).astype(BF16)
-    near[...] = jnp.zeros_like(near)
-
-    barrier = pltpu.get_barrier_semaphore()
-    for k in range(1, z.nsp):
-        pl.semaphore_signal(barrier, inc=1, device_id=((me + k) % z.nsp, my), device_id_type=MESH)
-    for k in range(1, z.nhd):
-        pl.semaphore_signal(barrier, inc=1, device_id=(me, (my + k) % z.nhd), device_id_type=MESH)
-
-    def inside(dr, dc):
-        ok = None
-        for step, at, count in ((dr, my, z.nhd), (dc, me, z.nsp)):
-            if step:
-                here = (at + step >= 0) & (at + step < count)
-                ok = here if ok is None else ok & here
-        return ok
-
-    greeted = z.nsp - 1 + z.nhd - 1
-    for dr in (-1, 1):
-        for dc in (-1, 1):
-
-            @pl.when(inside(dr, dc))
-            def _():
-                pl.semaphore_signal(barrier, inc=1, device_id=(me + dc, my + dr), device_id_type=MESH)
-
-            greeted = greeted + inside(dr, dc).astype(jnp.int32)
     pl.semaphore_wait(barrier, greeted)
 
     def gather_start(buf, phase):
@@ -176,21 +175,39 @@
             if z.span > z.tp:
                 part = jnp.concatenate([part, jnp.zeros((z.span - z.tp, z.lanes), F32)], axis=0)
             buf[pl.ds(half * z.keys + z.cache, z.span), :] = part.astype(BF16)
-    for copy in loads[:attention_loads]:
-        copy.wait()
-    sent = gather_finish(g, 0, first)
+    out_rows, in_rows = z.nsp * z.message, z.nsp * z.tp
+    out_at, in_at = iota((out_rows, in_rows), 0), iota((out_rows, in_rows), 1)
+    out_sp, inner = out_at // z.message, out_at % z.message
+    wanted = in_at == ((out_sp % 2) * nchip + out_sp // 2) * z.tp + inner % z.slot
+    for piece in range(z.pieces):
+        picked = jnp.where(wanted & (inner // z.slot == piece), 1.0, 0.0).astype(BF16)
+        pick_out[:, pl.ds(piece * in_rows, in_rows)] = picked
+    to_rows, from_rows = z.nsp * 8, z.nsp * z.message
+    to_at, from_at = iota((to_rows, from_rows), 0), iota((to_rows, from_rows), 1)
+    wanted = from_at - (to_at // 8) * z.message - to_at % 8
+    for piece in range(z.pieces):
+        picked = (wanted == piece * z.slot) & (to_at % 8 < z.slot)
+        pick_in[pl.ds(piece * to_rows, to_rows), :] = jnp.where(picked, 1.0, 0.0).astype(BF16)
 
     chunk = min(z.all, 256)
     total_keys = z.halves * z.keys
     lane = iota((chunk, LANES), 1)
     scale = 1.0 / math.sqrt(HDIM)
-    mask = valid_ref[...] > 0.0
+    key = iota((1, z.keys), 1)
+    live = jnp.where(age_ref[...][None, :] < history_ref[0], 1.0, 0.0).astype(F32)
+    live = jnp.concatenate([live, jnp.zeros((1, z.span), F32)], axis=1)
+    for slot, _, _ in z.slots():
+        live = jnp.where(key == z.cache + slot, 1.0, live)
+    bounds = [jnp.broadcast_to(live, (chunk, z.keys))] * z.halves
     if z.halves > 1:
-        row_half = (iota((chunk, total_keys), 0) // z.tp) % z.halves
-        col_half = (iota((chunk, total_keys), 1) >= z.keys).astype(jnp.int32)
-        mask = mask & (row_half == col_half)
-    else:
-        mask = jnp.broadcast_to(mask, (chunk, total_keys))
+        row_half = (iota((chunk, z.keys), 0) // z.tp) % z.halves
+        bounds = [jnp.where(row_half == half, b, 0.0) for half, b in enumerate(bounds)]
+    mask = jnp.concatenate(bounds, axis=1) > 0.0
+    ones = jnp.ones((total_keys, LANES), BF16)
+
+    for copy in loads[:attention_loads]:
+        copy.wait()
+    sent = gather_finish(g, 0, first)
 
     def attend(at, carry):
         rows = pl.ds(pl.multiple_of(at * chunk, chunk), chunk)
@@ -203,9 +220,11 @@
             scores = jnp.where(mask, scores * scale, -1e30)
             top = jnp.max(scores, axis=1, keepdims=True)
             weights = jnp.exp(scores - top).astype(BF16)
-            total = jnp.sum(weights.astype(F32), axis=1, keepdims=True)
-            out = jnp.dot(weights, v2[:, cols], preferred_element_type=F32)
-            o[rows, cols] = out.astype(BF16)
+            out = jnp.dot(
+                weights, jnp.concatenate([v2[:, cols], ones], axis=1), preferred_element_type=F32
+            )
+            total = out[:, HDIM:]
+            o[rows, cols] = out[:, :HDIM].astype(BF16)
             stats = jnp.where(lane == j, top, jnp.where(lane == j + 64, total, stats))
         st[rows, :] = stats
         return carry
@@ -275,26 +294,26 @@
     everything = att[...]
     proj = None
     for half in range(z.halves):
-        term = jnp.dot(everything, w[pl.ds(half * z.lanes, z.lanes), :], preferred_element_type=F32)
+        term = lax.dot_general(
+            everything, w[:, pl.ds(half * z.lanes, z.lanes)], (((1,), (1,)), ((), ())),
+            preferred_element_type=F32,
+        )
         term = term.reshape(z.nsp, z.halves, z.tp, z.part)[:, half]
         proj = term if proj is None else proj + term
-    proj = proj.reshape(z.nsp * z.tp, z.part).astype(BF16)
-    out_rows, in_rows = z.nsp * z.message, z.nsp * z.tp
-    out_at, in_at = iota((out_rows, in_rows), 0), iota((out_rows, in_rows), 1)
-    out_sp, inner = out_at // z.message, out_at % z.message
-    base = ((out_sp % 2) * nchip + out_sp // 2) * z.tp + inner % z.slot
+    proj = proj.reshape(z.nsp * z.tp, z.part)
+    wide = z.pieces * LANES
+    if wide > z.part:
+        proj = jnp.concatenate([proj, jnp.zeros((in_rows, wide - z.part), F32)], axis=1)
+    owned = []
     for owner in range(z.nhd):
-        wanted = in_at == base + owner * z.slot
-        cells = []
-        moved = jnp.zeros((out_rows, LANES), F32)
-        for piece in range(z.pieces):
-            wide = min(LANES, z.part - piece * LANES)
-            pick = jnp.where(wanted & (inner // z.slot == piece), 1.0, 0.0).astype(BF16)
-            got = jnp.dot(pick, proj[:, piece * LANES : piece * LANES + wide], preferred_element_type=F32)
-            if wide < LANES:
-                got = jnp.concatenate([got, jnp.zeros((out_rows, LANES - wide), F32)], axis=1)
-            moved = moved + got
-        zs[owner] = moved.astype(BF16)
+        turned = pltpu.roll(proj, in_rows - owner * z.slot, 0) if owner else proj
+        turned = turned.astype(BF16)
+        owned.append(
+            jnp.concatenate([turned[:, i * LANES : (i + 1) * LANES] for i in range(z.pieces)], axis=0)
+        )
+    moved = jnp.dot(pick_out[...], jnp.concatenate(owned, axis=1), preferred_element_type=F32).astype(BF16)
+    for owner in range(z.nhd):
+        zs[owner] = moved[:, owner * LANES : (owner + 1) * LANES]
 
     swaps = []
     for k in range(1, z.nhd):
@@ -325,13 +344,8 @@
     for copy in spread:
         copy.wait_recv()
 
-    got_all = r_got[...]
-    to_rows, from_rows = z.nsp * 8, z.nsp * z.message
-    to_at, from_at = iota((to_rows, from_rows), 0), iota((to_rows, from_rows), 1)
-    by_piece = []
-    for piece in range(z.pieces):
-        pick = (from_at == (to_at // 8) * z.message + piece * z.slot + to_at % 8) & (to_at % 8 < z.slot)
-        by_piece.append(jnp.dot(jnp.where(pick, 1.0, 0.0).astype(BF16), got_all, preferred_element_type=F32))
+    picked = jnp.dot(pick_in[...], r_got[...], preferred_element_type=F32)
+    by_piece = [picked[i * to_rows : (i + 1) * to_rows] for i in range(z.pieces)]
     lane8 = iota((8, LANES), 1)
     row8 = iota((8, LANES), 0)
     tiles = []
@@ -352,10 +366,11 @@
         cols = pl.ds(begin, LANES)
         base_value = jnp.zeros((8, LANES), F32)
         for f in range(z.frames):
-            base_value = jnp.where(row8 == f, stream_ref[f, :, cols].astype(F32), base_value)
+            base_value = jnp.where(row8 == f, stream_ref[f : f + 1, cols].astype(F32), base_value)
         value = base_value + gate_ref[:, cols] * value
-        value = value.astype(BF16).astype(F32)
-        so_ref[:, cols] = value
+        rounded = value.astype(BF16)
+        so_ref[:, cols] = rounded[: z.frames]
+        value = rounded.astype(F32)
         tiles.append(value)
     mean = jnp.sum(functools.reduce(jnp.add, tiles), axis=1, keepdims=True) / z.model
     centred = [t - mean for t in tiles]
@@ -367,11 +382,18 @@
         normed.append(t * root * (1.0 + scale_ref[:, cols]) + shift_ref[:, cols])
     normed = jnp.concatenate(normed, axis=1)
     normed = jnp.concatenate([normed, jnp.zeros_like(normed)], axis=0).astype(BF16)
-    patch = jnp.dot(normed, hw[...], preferred_element_type=F32)
+    patch = lax.dot_general(
+        normed, hw[...], (((1,), (1,)), ((), ())), preferred_element_type=F32
+    )
     cells = patch.shape[1]
     past = latc_ref.shape[0]
     tmp[...] = jnp.zeros_like(tmp)
-    tmp[0:past, 0:cells] = latc_ref[...]
+    chan = cells // 4
+    for f in range(past):
+        for a in range(2):
+            for b in range(2):
+                at = (a * 2 + b) * chan
+                tmp[f : f + 1, at : at + chan] = latc_ref[f, a, b : b + 1, :].astype(F32)
     tmp[past : past + z.frames, 0:cells] = patch[0 : z.frames]
     msg[...] = tmp[...].astype(BF16)
 
@@ -403,7 +425,6 @@
             ).wait_recv()
 
     around = [near[i].astype(F32)[0:8] for i in range(9)]
-    chan = cells // 4
     taps = 9 * chan
     wide_taps, rest_taps = [], []
     for i in range(2):
@@ -431,35 +452,39 @@
             jnp.dot(wide_taps, cw[pl.ds(u * taps, LANES), :], preferred_element_type=F32)
             + jnp.dot(rest_taps, cw[pl.ds(u * taps + LANES, taps - LANES), :], preferred_element_type=F32)
         )
+    gain = gain_ref[...][None, :]
+    decoded = []
     for cell in range(4):
         rows = slice(cell * 8, cell * 8 + 8)
         conv = steps[0][rows] + pltpu.roll(steps[1][rows], 7, 0) + pltpu.roll(steps[2][rows], 6, 0)
         square = jnp.sum(conv * conv, axis=1, keepdims=True) / conv.shape[1]
-        scaled = conv * lax.rsqrt(square + 1e-6) * gain_ref[...]
-        dec_ref[cell] = scaled / (1.0 + jnp.exp(-scaled))
+        scaled = conv * lax.rsqrt(square + 1e-6) * gain
+        decoded.append(scaled / (1.0 + jnp.exp(-scaled)))
+    for f in range(z.frames):
+        for i in range(2):
+            pair_of = [decoded[i * 2 + j][f : f + 1] for j in range(2)]
+            dec_ref[f, i] = jnp.concatenate(pair_of, axis=0).astype(BF16)
 
 
 def local(
     mesh, stream, queries, span_k, span_v, cache_k, cache_v, cache_age, history, out_weight,
     attn_gate, head_shift, head_scale, head_weight, latent_cache, conv_weight, rms_gain,
 ):
+    queries, span_k, span_v = (t[:, :, 0] for t in (queries, span_k, span_v))
+    out_weight, head_weight = out_weight.T, head_weight.T
     z = Sizes(mesh, queries, cache_k, out_weight)
-    span_valid = np.zeros((z.span,), np.float32)
-    for slot, _, _ in z.slots():
-        span_valid[slot] = 1.0
-    valid = jnp.concatenate([jnp.where(cache_age < history[0], 1.0, 0.0).astype(F32), jnp.asarray(span_valid)])
-    valid = jnp.tile(valid, z.halves)[None, :]
     model, chan = z.model, conv_weight.shape[1]
-    past = latent_cache.shape[0]
-    latc = latent_cache.reshape(past, -1).astype(F32)
     vmem = pl.BlockSpec(memory_space=pltpu.VMEM)
     hbm = pl.BlockSpec(memory_space=pl.ANY)
     half = z.all // 2
     dma = lambda *shape: pltpu.SemaphoreType.DMA(shape)
     out, dec = pl.pallas_call(
         functools.partial(kernel, z),
-        out_shape=(jax.ShapeDtypeStruct((8, model), F32), jax.ShapeDtypeStruct((4, 8, chan), F32)),
-        in_specs=[vmem] * 10 + [hbm] * 5,
+        out_shape=(
+            jax.ShapeDtypeStruct((z.frames, model), BF16),
+            jax.ShapeDtypeStruct((z.frames, 2, 2, chan), BF16),
+        ),
+        in_specs=[vmem] * 4 + [pl.BlockSpec(memory_space=pltpu.SMEM)] + [vmem] * 6 + [hbm] * 5,
         out_specs=(vmem, vmem),
         scratch_shapes=[
             pltpu.VMEM((z.all, z.lanes), BF16),
@@ -484,6 +509,8 @@
             pltpu.VMEM((9, 16, LANES), BF16),
             pltpu.VMEM((16, LANES), BF16),
             pltpu.VMEM((16, LANES), F32),
+            pltpu.VMEM((z.nsp * z.message, z.pieces * z.nsp * z.tp), BF16),
+            pltpu.VMEM((z.pieces * z.nsp * 8, z.nsp * z.message), BF16),
             dma(2 * z.halves + 3),
             dma(2, z.nchip), dma(2, z.nchip), dma(2, z.nchip), dma(2, z.nchip),
             dma(2), dma(2),
@@ -497,13 +524,11 @@
         ),
         name="span_block",
     )(
-        queries, span_k, span_v, valid, stream.reshape(z.frames, 1, model),
-        attn_gate[None], head_shift[None], head_scale[None], latc, rms_gain[None],
+        queries, span_k, span_v, cache_age, history, stream.reshape(z.frames, model),
+        attn_gate[None], head_shift[None], head_scale[None], latent_cache, rms_gain,
         cache_k, cache_v, out_weight, head_weight, conv_weight,
     )
-    stream_out = out[: z.frames].astype(BF16).reshape(stream.shape)
-    decoded = jnp.transpose(dec.reshape(2, 2, 8, chan)[:, :, : z.frames], (2, 0, 1, 3)).astype(BF16)
-    return stream_out, decoded
+    return out.reshape(stream.shape), dec
 
 
 def solution(mesh):

time: 73.7 us -> 57.8 us (0.78)
  local copies, waits for them, and re-layouts: 15.8 us -> 2.72 us
  other arithmetic: 2.19 us -> 0 us
    unnamed x8 -> x2, local copies, waits for them, and re-layouts: 9.57 us -> 2.72 us
    reshape x2 -> x0, local copies, waits for them, and re-layouts: 2.99 us -> none  [the longest x1 1.55 us: local(): stream_out = out[:z.frames].astype(BF16).reshape(stream.shape)]
    convert_element_type x1 -> x0, local copies, waits for them, and re-layouts: 1.3 us -> none  [local(): latc = latent_cache.reshape(past, -1).astype(F32)]
    broadcast_in_dim x1 -> x0, local copies, waits for them, and re-layouts: 1.24 us -> none  [local(): rms_gain[None]]
    another operation x1 -> x0, other arithmetic: 0.8 us -> none
where the time goes in v2:
time: 57.8 us; the launch traced here: 57.1 us
  Pallas kernels  53.1 us (92%)
  local copies, waits for them, and re-layouts  2.72 us (5%)
  between operations  1.29 us (2%)
    pallas_call x1, Pallas kernels, local(): pl.pallas_call(functools.partial(kernel, z), out_shape=(jax.ShapeDtypeStr...  53.1 us
    unnamed x2, local copies, waits for them, and re-layouts  2.72 us

profile of v2, /device:TPU:1, one launch (start us, length us, event | category | flops | bytes accessed | tf_op | source)
XLA Modules:
  0.0 57.1 jit_solution(11755375205435154287)
XLA Ops:
  1.3 53.1 %span_block.1 = (bf16[3,5120]{1,0:T(4,128)(2,1)}, bf16[3,2,2,384]{3,2,1,0:T(2,128)(2,1)}) custom-call(bf16[3,2,2560]{2,1,0:T(2,128)(2,1)} %bitcast.14, bf16[3,2,2560]{2,1,0:T(2,128)(2,1)} %bitcast.15, bf16[3,2,2560]{2,1,0:T(2,128)(2,1)} %bitcast.16, s32[96]{0:T(128)} %age_ref.1, s32[1]{0:T(128)S(6)} %copy.20.history_ref, bf16[3,5120]{1,0:T(4,128)(2,1)} %bitcast.12, ...), custom_call_target="tpu_custom_call" | custom-call | tf_op jit(solution)/shard_map/span_block/pallas_call | solution.py:481
  54.4 1.4 %copy.21 = bf16[3,1,1,5120]{3,0,2,1:T(4,128)(2,1)} copy(bf16[3,1,1,5120]{3,0,2,1:T(4,128)(2,1)} %bitcast.13) | data formatting | bytes 61440
  55.8 1.3 %copy.22 = bf16[3,2,2,384]{3,2,1,0:T(2,128)(2,1)} copy(bf16[3,2,2,384]{3,2,1,0:T(2,128)(2,1)} %get-tuple-element.9) | data formatting | bytes 18432

commit v3 on v2

--- a/solution.py
+++ b/solution.py
@@ -35,6 +35,9 @@
         self.block = self.halves * self.tp
         self.lanes = self.width // self.halves
         self.pairs = self.heads // self.halves
+        self.chunks = 1 if self.pairs % 2 else 2
+        self.chunk_pairs = self.pairs // self.chunks
+        self.wide = self.lanes // self.chunks
         self.cache = cache_k.shape[0]
         self.keys = up(self.cache + up(self.tp, 16), LANES)
         self.span = self.keys - self.cache
@@ -67,8 +70,8 @@
     z, q_ref, k_ref, v_ref, age_ref, history_ref, stream_ref, gate_ref, shift_ref, scale_ref, latc_ref, gain_ref,
     ck_hbm, cv_hbm, w_hbm, hw_hbm, cw_hbm,
     so_ref, dec_ref,
-    g, att, o, st, o_in, s_in, co, cs, o_got, s_got, k2, v2, w, hw, cw, zs, z_got, h, r_got, near, msg, tmp, pick_out, pick_in,
-    local_sem, ag_send, ag_recv, fw_send, fw_recv, sib_send, sib_recv, b_send, b_recv,
+    g, att, o, o_in, co, o_got, k2, v2, w, hw, cw, zs, z_got, h, r_got, near, msg, tmp, pick_out, pick_in,
+    local_sem, z_send, z_recv, x_send, x_recv, c_send, c_recv, sib_send, sib_recv, b_send, b_recv,
     hd_send, hd_recv, e_send, e_recv, n_send, n_recv,
 ):
     me, my = lax.axis_index("sp"), lax.axis_index("hd")
@@ -142,34 +145,56 @@
     load(hw_hbm, hw)
     load(cw_hbm, cw)
 
-    g[rows_of(core, chip), :] = jnp.concatenate(packed(q_ref), axis=0).astype(BF16)
+    mine_q = jnp.concatenate(packed(q_ref), axis=0).astype(BF16)
+    for ch in range(z.chunks):
+        g[ch, rows_of(core, chip), :] = mine_q[:, ch * z.wide : (ch + 1) * z.wide]
     pl.semaphore_wait(barrier, greeted)
 
-    def gather_start(buf, phase):
-        mine = rows_of(core, chip)
-        first = [
-            remote(buf.at[mine], buf.at[mine], ag_send.at[phase, k], ag_recv.at[phase, k],
-                   peer(k) * 2 + core, my)
-            for k in range(1, nchip)
-        ]
-        for copy in first:
-            copy.start()
-        return first
-
-    def gather_finish(buf, phase, first):
-        forwards = []
-        for k in range(nchip):
-            if k:
-                first[k - 1].wait_recv()
-            rows = rows_of(core, source(k))
-            copy = remote(buf.at[rows], buf.at[rows], fw_send.at[phase, k], fw_recv.at[phase, k], sib, my)
-            copy.start()
-            forwards.append(copy)
-        for copy in forwards:
-            copy.wait_recv()
-        return first + forwards
-
-    first = gather_start(g, 0)
+    far, side = nchip // 2, chip % 2
+    partner = (chip + 1 - 2 * side) * 2 + core
+    pending = []
+
+    def distant(k):
+        return (chip // 2 + far - k) % far
+
+    def pass_on(buf, phase, ch, at_core, at_chip, sems, slot, to):
+        rows = rows_of(at_core, at_chip)
+        ssem, rsem = sems
+        copy = remote(buf.at[ch, rows], buf.at[ch, rows], ssem.at[phase, ch, slot], rsem.at[phase, ch, slot], to, my)
+        copy.start()
+        pending.append(copy)
+        return copy
+
+    along, across, within = (z_send, z_recv), (x_send, x_recv), (c_send, c_recv)
+
+    class Gather:
+        def __init__(self, buf, phase, ch):
+            self.at = (buf, phase, ch)
+            self.z = [
+                pass_on(*self.at, core, chip, along, k, (((chip // 2 + k) % far) * 2 + side) * 2 + core)
+                for k in range(1, far)
+            ]
+            self.x = [pass_on(*self.at, core, chip, across, 0, partner)]
+            self.c = [pass_on(*self.at, core, chip, within, 0, sib)]
+
+        def relay_z(self):
+            for k in range(1, far):
+                self.z[k - 1].wait_recv()
+                from_chip = distant(k) * 2 + side
+                self.x.append(pass_on(*self.at, core, from_chip, across, k, partner))
+                self.c.append(pass_on(*self.at, core, from_chip, within, k, sib))
+
+        def relay_x(self):
+            for k in range(far):
+                self.x[k].wait_recv()
+                from_chip = distant(k) * 2 + 1 - side
+                self.c.append(pass_on(*self.at, core, from_chip, within, far + k, sib))
+
+        def finish(self):
+            for copy in self.c:
+                copy.wait_recv()
+
+    asked = [Gather(g, 0, ch) for ch in range(z.chunks)]
     for ref, buf in ((k_ref, k2), (v_ref, v2)):
         for half, part in enumerate(packed(ref)):
             if z.span > z.tp:
@@ -205,101 +230,126 @@
     mask = jnp.concatenate(bounds, axis=1) > 0.0
     ones = jnp.ones((total_keys, LANES), BF16)
 
+    asked[0].relay_z()
     for copy in loads[:attention_loads]:
         copy.wait()
-    sent = gather_finish(g, 0, first)
-
-    def attend(at, carry):
-        rows = pl.ds(pl.multiple_of(at * chunk, chunk), chunk)
-        stats = jnp.zeros((chunk, LANES), F32)
-        for j in range(z.pairs):
-            cols = pl.ds(j * HDIM, HDIM)
-            scores = lax.dot_general(
-                g[rows, cols], k2[:, cols], (((1,), (1,)), ((), ())), preferred_element_type=F32
-            )
-            scores = jnp.where(mask, scores * scale, -1e30)
-            top = jnp.max(scores, axis=1, keepdims=True)
-            weights = jnp.exp(scores - top).astype(BF16)
-            out = jnp.dot(
-                weights, jnp.concatenate([v2[:, cols], ones], axis=1), preferred_element_type=F32
-            )
-            total = out[:, HDIM:]
-            o[rows, cols] = out[:, :HDIM].astype(BF16)
-            stats = jnp.where(lane == j, top, jnp.where(lane == j + 64, total, stats))
-        st[rows, :] = stats
-        return carry
-
-    lax.fori_loop(0, z.all // chunk, attend, 0)
+    asked[0].relay_x()
+    asked[0].finish()
+
+    def attend(ch, pairs):
+        def step(at, carry):
+            rows = pl.ds(pl.multiple_of(at * chunk, chunk), chunk)
+            stat_cols = pl.ds(z.wide, LANES)
+            stats = o[ch, rows, stat_cols].astype(F32) if pairs[0] else jnp.zeros((chunk, LANES), F32)
+            for j in pairs:
+                near_cols = pl.ds(j * HDIM, HDIM)
+                cols = pl.ds(ch * z.wide + j * HDIM, HDIM)
+                scores = lax.dot_general(
+                    g[ch, rows, near_cols], k2[:, cols], (((1,), (1,)), ((), ())), preferred_element_type=F32
+                )
+                scores = jnp.where(mask, scores * scale, -1e30)
+                top = jnp.max(scores, axis=1, keepdims=True).astype(BF16).astype(F32)
+                weights = jnp.exp(scores - top).astype(BF16)
+                out = jnp.dot(
+                    weights, jnp.concatenate([v2[:, cols], ones], axis=1), preferred_element_type=F32
+                )
+                o[ch, rows, near_cols] = out[:, :HDIM].astype(BF16)
+                stats = jnp.where(lane == j, top, jnp.where(lane == j + 64, out[:, HDIM:], stats))
+            o[ch, rows, stat_cols] = stats.astype(BF16)
+            return carry
+
+        if z.all == chunk:
+            step(0, 0)
+        else:
+            lax.fori_loop(0, z.all // chunk, step, 0)
 
     half_rows = nchip * block
     theirs = pl.ds(pl.multiple_of((1 - core) * half_rows, half_rows), half_rows)
-    pair = [
-        remote(st.at[theirs], s_in, sib_send.at[0], sib_recv.at[0], sib, my),
-        remote(o.at[theirs], o_in, sib_send.at[1], sib_recv.at[1], sib, my),
-    ]
-    for copy in pair:
+    low = iota((block, LANES), 1) < 64
+
+    def give(ch):
+        copy = remote(o.at[ch, theirs], o_in.at[ch], sib_send.at[ch], sib_recv.at[ch], sib, my)
         copy.start()
-    for copy in sent:
-        copy.wait_send()
-    for copy in pair:
-        copy.wait_recv()
-
-    low = iota((block, LANES), 1) < 64
-    exchanged = []
-    for k in list(range(1, nchip)) + [0]:
-        to = peer(k)
-        mine, rows = rows_of(core, to), chip_rows(to)
-        top, total, (a, b) = merge_stats([st[mine, :], s_in[rows, :]])
-        cs[rows, :] = jnp.where(low, top, total)
-        for j in range(z.pairs):
-            cols = pl.ds(j * HDIM, HDIM)
-            merged = (
-                o[mine, cols].astype(F32) * a[:, j : j + 1]
-                + o_in[rows, cols].astype(F32) * b[:, j : j + 1]
+        pending.append(copy)
+        return copy
+
+    def merge(ch, given):
+        given.wait_recv()
+        stat_cols = pl.ds(z.wide, LANES)
+        copies = []
+        for k in list(range(1, nchip)) + [0]:
+            to = peer(k)
+            mine, rows = rows_of(core, to), chip_rows(to)
+            top, total, (a, b) = merge_stats(
+                [o[ch, mine, stat_cols].astype(F32), o_in[ch, rows, stat_cols].astype(F32)]
             )
-            co[rows, cols] = merged.astype(BF16)
-        if k:
-            there = chip_rows(chip)
-            for which, (src, dst) in enumerate(((cs, s_got), (co, o_got))):
-                copy = remote(src.at[rows], dst.at[there], b_send.at[which, k], b_recv.at[which, k],
+            dst, at = (co, rows) if k else (o_got, chip_rows(chip))
+            dst[ch, at, stat_cols] = jnp.where(low, top, total).astype(BF16)
+            for j in range(z.chunk_pairs):
+                cols = pl.ds(j * HDIM, HDIM)
+                merged = (
+                    o[ch, mine, cols].astype(F32) * a[:, j : j + 1]
+                    + o_in[ch, rows, cols].astype(F32) * b[:, j : j + 1]
+                )
+                dst[ch, at, cols] = merged.astype(BF16)
+            if k:
+                copy = remote(co.at[ch, rows], o_got.at[ch, chip_rows(chip)], b_send.at[ch, k], b_recv.at[ch, k],
                               to * 2 + core, my)
                 copy.start()
-                exchanged.append(copy)
-    own_rows = chip_rows(chip)
-    s_got[own_rows, :] = cs[own_rows, :]
-    o_got[own_rows, :] = co[own_rows, :]
-    for copy in exchanged:
-        copy.wait_recv()
-
-    top, total, scales = merge_stats([s_got[pl.ds(i * block, block), :] for i in range(nchip)])
-    inverse = pltpu.roll(1.0 / jnp.where(low, 1.0, total), 64, 1)
-    for j in range(z.pairs):
-        cols = pl.ds(j * HDIM, HDIM)
-        summed = functools.reduce(
-            jnp.add,
-            [
-                o_got[pl.ds(i * block, block), cols].astype(F32) * scales[i][:, j : j + 1]
-                for i in range(nchip)
-            ],
-        )
-        att[rows_of(core, chip), cols] = (summed * inverse[:, j : j + 1]).astype(BF16)
-
-    first = gather_start(att, 1)
-    for copy in pair + exchanged:
-        copy.wait_send()
+                copies.append(copy)
+        pending.extend(copies)
+        return copies
+
+    def settle(ch, copies):
+        for copy in copies:
+            copy.wait_recv()
+        parts = [pl.ds(i * block, block) for i in range(nchip)]
+        top, total, scales = merge_stats([o_got[ch, p, pl.ds(z.wide, LANES)].astype(F32) for p in parts])
+        inverse = pltpu.roll(1.0 / jnp.where(low, 1.0, total), 64, 1)
+        for j in range(z.chunk_pairs):
+            cols = pl.ds(j * HDIM, HDIM)
+            terms = [o_got[ch, p, cols].astype(F32) * s[:, j : j + 1] for p, s in zip(parts, scales)]
+            summed = functools.reduce(jnp.add, terms)
+            att[ch, rows_of(core, chip), cols] = (summed * inverse[:, j : j + 1]).astype(BF16)
+        return Gather(att, 1, ch)
+
+    cut = max(1, z.chunk_pairs // 2)
+    first_pairs, last_pairs = range(cut), range(cut, z.chunk_pairs)
+    given, partials, shared = [], [], []
+    for ch in range(z.chunks):
+        if ch:
+            asked[ch].finish()
+        more = ch + 1 < z.chunks
+        if more:
+            asked[ch + 1].relay_z()
+        attend(ch, first_pairs)
+        if ch:
+            partials.append(merge(ch - 1, given[ch - 1]))
+        if more:
+            asked[ch + 1].relay_x()
+        attend(ch, last_pairs)
+        given.append(give(ch))
+    partials.append(merge(z.chunks - 1, given[-1]))
+    for ch in range(z.chunks):
+        shared.append(settle(ch, partials[ch]))
+        if ch:
+            shared[ch - 1].relay_x()
+        shared[ch].relay_z()
+    shared[-1].relay_x()
+
     for copy in loads[attention_loads:]:
         copy.wait()
-    sent = gather_finish(att, 1, first)
-
-    everything = att[...]
-    proj = None
-    for half in range(z.halves):
-        term = lax.dot_general(
-            everything, w[:, pl.ds(half * z.lanes, z.lanes)], (((1,), (1,)), ((), ())),
-            preferred_element_type=F32,
-        )
-        term = term.reshape(z.nsp, z.halves, z.tp, z.part)[:, half]
-        proj = term if proj is None else proj + term
+    proj = [None] * z.halves
+    for ch in range(z.chunks):
+        shared[ch].finish()
+        for half in range(z.halves):
+            term = lax.dot_general(
+                att[ch], w[:, pl.ds(half * z.lanes + ch * z.wide, z.wide)], (((1,), (1,)), ((), ())),
+                preferred_element_type=F32,
+            )
+            proj[half] = term if proj[half] is None else proj[half] + term
+    picked = [p.reshape(z.nsp, z.halves, z.tp, z.part)[:, half] for half, p in enumerate(proj)]
+    proj = functools.reduce(jnp.add, picked)
     proj = proj.reshape(z.nsp * z.tp, z.part)
     wide = z.pieces * LANES
     if wide > z.part:
@@ -321,8 +371,6 @@
         copy = remote(zs.at[to], z_got.at[my], hd_send.at[k], hd_recv.at[k], me, to)
         copy.start()
         swaps.append(copy)
-    for copy in sent:
-        copy.wait_send()
     summed = zs[my].astype(F32)
     for k in range(1, z.nhd):
         swaps[k - 1].wait_recv()
@@ -339,8 +387,8 @@
         copy.start()
         spread.append(copy)
     r_got[message_rows(me), :] = h[message_rows(me), :]
-    for copy in swaps:
-        copy.wait_send()
+    pending.extend(swaps)
+    pending.extend(spread)
     for copy in spread:
         copy.wait_recv()
 
@@ -410,8 +458,6 @@
             halo(dr, dc).start()
 
     near[4] = msg[...]
-    for copy in spread:
-        copy.wait_send()
     for dr, dc in order:
 
         @pl.when(inside(dr, dc))
@@ -452,6 +498,8 @@
             jnp.dot(wide_taps, cw[pl.ds(u * taps, LANES), :], preferred_element_type=F32)
             + jnp.dot(rest_taps, cw[pl.ds(u * taps + LANES, taps - LANES), :], preferred_element_type=F32)
         )
+    for copy in pending:
+        copy.wait_send()
     gain = gain_ref[...][None, :]
     decoded = []
     for cell in range(4):
@@ -487,16 +535,12 @@
         in_specs=[vmem] * 4 + [pl.BlockSpec(memory_space=pltpu.SMEM)] + [vmem] * 6 + [hbm] * 5,
         out_specs=(vmem, vmem),
         scratch_shapes=[
-            pltpu.VMEM((z.all, z.lanes), BF16),
-            pltpu.VMEM((z.all, z.lanes), BF16),
-            pltpu.VMEM((z.all, z.lanes), BF16),
-            pltpu.VMEM((z.all, LANES), F32),
-            pltpu.VMEM((half, z.lanes), BF16),
-            pltpu.VMEM((half, LANES), F32),
-            pltpu.VMEM((half, z.lanes), BF16),
-            pltpu.VMEM((half, LANES), F32),
-            pltpu.VMEM((half, z.lanes), BF16),
-            pltpu.VMEM((half, LANES), F32),
+            pltpu.VMEM((z.chunks, z.all, z.wide), BF16),
+            pltpu.VMEM((z.chunks, z.all, z.wide), BF16),
+            pltpu.VMEM((z.chunks, z.all, z.wide + LANES), BF16),
+            pltpu.VMEM((z.chunks, half, z.wide + LANES), BF16),
+            pltpu.VMEM((z.chunks, half, z.wide + LANES), BF16),
+            pltpu.VMEM((z.chunks, half, z.wide + LANES), BF16),
             pltpu.VMEM((z.halves * z.keys, z.lanes), BF16),
             pltpu.VMEM((z.halves * z.keys, z.lanes), BF16),
             pltpu.VMEM(out_weight.shape, BF16),
@@ -512,9 +556,11 @@
             pltpu.VMEM((z.nsp * z.message, z.pieces * z.nsp * z.tp), BF16),
             pltpu.VMEM((z.pieces * z.nsp * 8, z.nsp * z.message), BF16),
             dma(2 * z.halves + 3),
-            dma(2, z.nchip), dma(2, z.nchip), dma(2, z.nchip), dma(2, z.nchip),
-            dma(2), dma(2),
-            dma(2, z.nchip), dma(2, z.nchip),
+            dma(2, z.chunks, z.nchip), dma(2, z.chunks, z.nchip),
+            dma(2, z.chunks, z.nchip), dma(2, z.chunks, z.nchip),
+            dma(2, z.chunks, z.nchip), dma(2, z.chunks, z.nchip),
+            dma(z.chunks), dma(z.chunks),
+            dma(z.chunks, z.nchip), dma(z.chunks, z.nchip),
             dma(z.nhd), dma(z.nhd),
             dma(z.nsp), dma(z.nsp),
             dma(9), dma(9),

time: 57.8 us -> 60.2 us (1.042)
  Pallas kernels: 53.1 us -> 55.9 us
    pallas_call x1, Pallas kernels: 53.1 us -> 55.9 us  [local(): pl.pallas_call(functools.partial(kernel, z), out_shape=(jax.ShapeDtypeStr...]
where the time goes in v3:
time: 60.2 us; the launch traced here: 59.9 us
  Pallas kernels  55.9 us (93%)
  local copies, waits for them, and re-layouts  2.72 us (5%)
  between operations  1.29 us (2%)
    pallas_call x1, Pallas kernels, local(): pl.pallas_call(functools.partial(kernel, z), out_shape=(jax.ShapeDtypeStr...  55.9 us
    unnamed x2, local copies, waits for them, and re-layouts  2.72 us

profile of v3, /device:TPU:1, one launch (start us, length us, event | category | flops | bytes accessed | tf_op | source)
XLA Modules:
  0.0 59.9 jit_solution(14535229710603125204)
XLA Ops:
  1.3 55.9 %span_block.1 = (bf16[3,5120]{1,0:T(4,128)(2,1)}, bf16[3,2,2,384]{3,2,1,0:T(2,128)(2,1)}) custom-call(bf16[3,2,2560]{2,1,0:T(2,128)(2,1)} %bitcast.14, bf16[3,2,2560]{2,1,0:T(2,128)(2,1)} %bitcast.15, bf16[3,2,2560]{2,1,0:T(2,128)(2,1)} %bitcast.16, s32[96]{0:T(128)} %age_ref.1, s32[1]{0:T(128)S(6)} %copy.20.history_ref, bf16[3,5120]{1,0:T(4,128)(2,1)} %bitcast.12, ...), custom_call_target="tpu_custom_call" | custom-call | tf_op jit(solution)/shard_map/span_block/pallas_call | solution.py:529
  57.2 1.4 %copy.21 = bf16[3,1,1,5120]{3,0,2,1:T(4,128)(2,1)} copy(bf16[3,1,1,5120]{3,0,2,1:T(4,128)(2,1)} %bitcast.13) | data formatting | bytes 61440
  58.6 1.3 %copy.22 = bf16[3,2,2,384]{3,2,1,0:T(2,128)(2,1)} copy(bf16[3,2,2,384]{3,2,1,0:T(2,128)(2,1)} %get-tuple-element.9) | data formatting | bytes 18432

commit v4 on v3

--- a/solution.py
+++ b/solution.py
@@ -53,6 +53,14 @@
                 yield (r // self.own) * self.slot + (r % self.own) * self.frames + f, f, r
 
 
+def div(value, by):
+    return value >> (by.bit_length() - 1) if by & (by - 1) == 0 else value // by
+
+
+def mod(value, by):
+    return value & (by - 1) if by & (by - 1) == 0 else value % by
+
+
 def iota(shape, dim):
     return lax.broadcasted_iota(jnp.int32, shape, dim)
 
@@ -70,7 +78,7 @@
     z, q_ref, k_ref, v_ref, age_ref, history_ref, stream_ref, gate_ref, shift_ref, scale_ref, latc_ref, gain_ref,
     ck_hbm, cv_hbm, w_hbm, hw_hbm, cw_hbm,
     so_ref, dec_ref,
-    g, att, o, o_in, co, o_got, k2, v2, w, hw, cw, zs, z_got, h, r_got, near, msg, tmp, pick_out, pick_in,
+    g, att, o, o_in, co, o_got, k2, v2, w, hw, cw, zs, z_got, h, r_got, near, msg, tmp, pick_out, pick_in, projected,
     local_sem, z_send, z_recv, x_send, x_recv, c_send, c_recv, sib_send, sib_recv, b_send, b_recv,
     hd_send, hd_recv, e_send, e_recv, n_send, n_recv,
 ):
@@ -85,11 +93,16 @@
     def source(k):
         return (chip + nchip - k) % nchip
 
+    far, side = nchip // 2, chip % 2
+
+    def place(which_chip):
+        return (which_chip % 2) * far + which_chip // 2
+
     def rows_of(which_core, which_chip):
-        return pl.ds(pl.multiple_of((which_core * nchip + which_chip) * block, block), block)
+        return pl.ds(pl.multiple_of((which_core * nchip + place(which_chip)) * block, block), block)
 
     def chip_rows(which_chip):
-        return pl.ds(pl.multiple_of(which_chip * block, block), block)
+        return pl.ds(pl.multiple_of(place(which_chip) * block, block), block)
 
     def remote(src, dst, ssem, rsem, sp, hd):
         return pltpu.make_async_remote_copy(
@@ -146,21 +159,18 @@
     load(cw_hbm, cw)
 
     mine_q = jnp.concatenate(packed(q_ref), axis=0).astype(BF16)
-    for ch in range(z.chunks):
-        g[ch, rows_of(core, chip), :] = mine_q[:, ch * z.wide : (ch + 1) * z.wide]
+    g[rows_of(core, chip), :] = mine_q
     pl.semaphore_wait(barrier, greeted)
 
-    far, side = nchip // 2, chip % 2
     partner = (chip + 1 - 2 * side) * 2 + core
     pending = []
 
     def distant(k):
         return (chip // 2 + far - k) % far
 
-    def pass_on(buf, phase, ch, at_core, at_chip, sems, slot, to):
-        rows = rows_of(at_core, at_chip)
+    def pass_on(buf, phase, rows, sems, slot, to):
         ssem, rsem = sems
-        copy = remote(buf.at[ch, rows], buf.at[ch, rows], ssem.at[phase, ch, slot], rsem.at[phase, ch, slot], to, my)
+        copy = remote(buf.at[rows], buf.at[rows], ssem.at[phase, slot], rsem.at[phase, slot], to, my)
         copy.start()
         pending.append(copy)
         return copy
@@ -168,33 +178,34 @@
     along, across, within = (z_send, z_recv), (x_send, x_recv), (c_send, c_recv)
 
     class Gather:
-        def __init__(self, buf, phase, ch):
-            self.at = (buf, phase, ch)
+        def __init__(self, buf, phase):
+            self.at = (buf, phase)
+            mine = rows_of(core, chip)
             self.z = [
-                pass_on(*self.at, core, chip, along, k, (((chip // 2 + k) % far) * 2 + side) * 2 + core)
+                pass_on(*self.at, mine, along, k, (((chip // 2 + k) % far) * 2 + side) * 2 + core)
                 for k in range(1, far)
             ]
-            self.x = [pass_on(*self.at, core, chip, across, 0, partner)]
-            self.c = [pass_on(*self.at, core, chip, within, 0, sib)]
-
-        def relay_z(self):
+            self.x = [pass_on(*self.at, mine, across, 0, partner)]
+            self.c = []
+
+        def batch(self, which_side):
+            rows = pl.ds(pl.multiple_of((core * 2 + which_side) * far * block, far * block), far * block)
+            self.c.append(pass_on(*self.at, rows, within, len(self.c), sib))
+
+        def relay(self):
             for k in range(1, far):
                 self.z[k - 1].wait_recv()
-                from_chip = distant(k) * 2 + side
-                self.x.append(pass_on(*self.at, core, from_chip, across, k, partner))
-                self.c.append(pass_on(*self.at, core, from_chip, within, k, sib))
-
-        def relay_x(self):
-            for k in range(far):
-                self.x[k].wait_recv()
-                from_chip = distant(k) * 2 + 1 - side
-                self.c.append(pass_on(*self.at, core, from_chip, within, far + k, sib))
+                self.x.append(pass_on(*self.at, rows_of(core, distant(k) * 2 + side), across, k, partner))
+            self.batch(side)
+            for copy in self.x:
+                copy.wait_recv()
+            self.batch(1 - side)
 
         def finish(self):
             for copy in self.c:
                 copy.wait_recv()
 
-    asked = [Gather(g, 0, ch) for ch in range(z.chunks)]
+    asked = Gather(g, 0)
     for ref, buf in ((k_ref, k2), (v_ref, v2)):
         for half, part in enumerate(packed(ref)):
             if z.span > z.tp:
@@ -202,19 +213,22 @@
             buf[pl.ds(half * z.keys + z.cache, z.span), :] = part.astype(BF16)
     out_rows, in_rows = z.nsp * z.message, z.nsp * z.tp
     out_at, in_at = iota((out_rows, in_rows), 0), iota((out_rows, in_rows), 1)
-    out_sp, inner = out_at // z.message, out_at % z.message
-    wanted = in_at == ((out_sp % 2) * nchip + out_sp // 2) * z.tp + inner % z.slot
+    out_sp, inner = div(out_at, z.message), mod(out_at, z.message)
+    at_chip = mod(out_sp, 2) * nchip + mod(div(out_sp, 2), 2) * far + div(out_sp, 4)
+    wanted = in_at == at_chip * z.tp + mod(inner, z.slot)
     for piece in range(z.pieces):
-        picked = jnp.where(wanted & (inner // z.slot == piece), 1.0, 0.0).astype(BF16)
+        picked = jnp.where(wanted & (div(inner, z.slot) == piece), 1.0, 0.0).astype(BF16)
         pick_out[:, pl.ds(piece * in_rows, in_rows)] = picked
     to_rows, from_rows = z.nsp * 8, z.nsp * z.message
     to_at, from_at = iota((to_rows, from_rows), 0), iota((to_rows, from_rows), 1)
-    wanted = from_at - (to_at // 8) * z.message - to_at % 8
+    to_slot = mod(to_at, 8)
+    wanted = from_at - div(to_at, 8) * z.message - to_slot
     for piece in range(z.pieces):
-        picked = (wanted == piece * z.slot) & (to_at % 8 < z.slot)
+        picked = (wanted == piece * z.slot) & (to_slot < z.slot)
         pick_in[pl.ds(piece * to_rows, to_rows), :] = jnp.where(picked, 1.0, 0.0).astype(BF16)
 
-    chunk = min(z.all, 256)
+    half_rows = nchip * block
+    chunk = min(half_rows, 256)
     total_keys = z.halves * z.keys
     lane = iota((chunk, LANES), 1)
     scale = 1.0 / math.sqrt(HDIM)
@@ -225,27 +239,25 @@
         live = jnp.where(key == z.cache + slot, 1.0, live)
     bounds = [jnp.broadcast_to(live, (chunk, z.keys))] * z.halves
     if z.halves > 1:
-        row_half = (iota((chunk, z.keys), 0) // z.tp) % z.halves
+        row_half = mod(div(iota((chunk, z.keys), 0), z.tp), z.halves)
         bounds = [jnp.where(row_half == half, b, 0.0) for half, b in enumerate(bounds)]
     mask = jnp.concatenate(bounds, axis=1) > 0.0
     ones = jnp.ones((total_keys, LANES), BF16)
 
-    asked[0].relay_z()
     for copy in loads[:attention_loads]:
         copy.wait()
-    asked[0].relay_x()
-    asked[0].finish()
-
-    def attend(ch, pairs):
+    asked.relay()
+
+    def attend(which_core, ch):
         def step(at, carry):
-            rows = pl.ds(pl.multiple_of(at * chunk, chunk), chunk)
+            rows = pl.ds(pl.multiple_of(which_core * half_rows + at * chunk, chunk), chunk)
             stat_cols = pl.ds(z.wide, LANES)
-            stats = o[ch, rows, stat_cols].astype(F32) if pairs[0] else jnp.zeros((chunk, LANES), F32)
-            for j in pairs:
+            stats = jnp.zeros((chunk, LANES), F32)
+            for j in range(z.chunk_pairs):
                 near_cols = pl.ds(j * HDIM, HDIM)
                 cols = pl.ds(ch * z.wide + j * HDIM, HDIM)
                 scores = lax.dot_general(
-                    g[ch, rows, near_cols], k2[:, cols], (((1,), (1,)), ((), ())), preferred_element_type=F32
+                    g[rows, cols], k2[:, cols], (((1,), (1,)), ((), ())), preferred_element_type=F32
                 )
                 scores = jnp.where(mask, scores * scale, -1e30)
                 top = jnp.max(scores, axis=1, keepdims=True).astype(BF16).astype(F32)
@@ -258,12 +270,11 @@
             o[ch, rows, stat_cols] = stats.astype(BF16)
             return carry
 
-        if z.all == chunk:
+        if half_rows == chunk:
             step(0, 0)
         else:
-            lax.fori_loop(0, z.all // chunk, step, 0)
-
-    half_rows = nchip * block
+            lax.fori_loop(0, half_rows // chunk, step, 0)
+
     theirs = pl.ds(pl.multiple_of((1 - core) * half_rows, half_rows), half_rows)
     low = iota((block, LANES), 1) < 64
 
@@ -310,47 +321,42 @@
             cols = pl.ds(j * HDIM, HDIM)
             terms = [o_got[ch, p, cols].astype(F32) * s[:, j : j + 1] for p, s in zip(parts, scales)]
             summed = functools.reduce(jnp.add, terms)
-            att[ch, rows_of(core, chip), cols] = (summed * inverse[:, j : j + 1]).astype(BF16)
-        return Gather(att, 1, ch)
-
-    cut = max(1, z.chunk_pairs // 2)
-    first_pairs, last_pairs = range(cut), range(cut, z.chunk_pairs)
-    given, partials, shared = [], [], []
+            cols = pl.ds(ch * z.wide + j * HDIM, HDIM)
+            att[rows_of(core, chip), cols] = (summed * inverse[:, j : j + 1]).astype(BF16)
+
     for ch in range(z.chunks):
-        if ch:
-            asked[ch].finish()
-        more = ch + 1 < z.chunks
-        if more:
-            asked[ch + 1].relay_z()
-        attend(ch, first_pairs)
-        if ch:
-            partials.append(merge(ch - 1, given[ch - 1]))
-        if more:
-            asked[ch + 1].relay_x()
-        attend(ch, last_pairs)
+        attend(core, ch)
+    asked.finish()
+    given = []
+    for ch in range(z.chunks):
+        attend(1 - core, ch)
         given.append(give(ch))
-    partials.append(merge(z.chunks - 1, given[-1]))
+    partials = [merge(ch, given[ch]) for ch in range(z.chunks)]
     for ch in range(z.chunks):
-        shared.append(settle(ch, partials[ch]))
-        if ch:
-            shared[ch - 1].relay_x()
-        shared[ch].relay_z()
-    shared[-1].relay_x()
+        settle(ch, partials[ch])
+    shared = Gather(att, 1)
+
+    def project(which_core):
+        part_rows = nchip * z.tp
+        tokens = att[pl.ds(pl.multiple_of(which_core * half_rows, half_rows), half_rows), :]
+        total = None
+        for half in range(z.halves):
+            term = lax.dot_general(
+                tokens, w[:, pl.ds(half * z.lanes, z.lanes)], (((1,), (1,)), ((), ())),
+                preferred_element_type=F32,
+            )
+            term = term.reshape(nchip, z.halves, z.tp, z.part)[:, half]
+            total = term if total is None else total + term
+        rows = pl.ds(pl.multiple_of(which_core * part_rows, part_rows), part_rows)
+        projected[rows, :] = total.reshape(part_rows, z.part)
 
     for copy in loads[attention_loads:]:
         copy.wait()
-    proj = [None] * z.halves
-    for ch in range(z.chunks):
-        shared[ch].finish()
-        for half in range(z.halves):
-            term = lax.dot_general(
-                att[ch], w[:, pl.ds(half * z.lanes + ch * z.wide, z.wide)], (((1,), (1,)), ((), ())),
-                preferred_element_type=F32,
-            )
-            proj[half] = term if proj[half] is None else proj[half] + term
-    picked = [p.reshape(z.nsp, z.halves, z.tp, z.part)[:, half] for half, p in enumerate(proj)]
-    proj = functools.reduce(jnp.add, picked)
-    proj = proj.reshape(z.nsp * z.tp, z.part)
+    shared.relay()
+    project(core)
+    shared.finish()
+    project(1 - core)
+    proj = projected[...]
     wide = z.pieces * LANES
     if wide > z.part:
         proj = jnp.concatenate([proj, jnp.zeros((in_rows, wide - z.part), F32)], axis=1)
@@ -535,8 +541,8 @@
         in_specs=[vmem] * 4 + [pl.BlockSpec(memory_space=pltpu.SMEM)] + [vmem] * 6 + [hbm] * 5,
         out_specs=(vmem, vmem),
         scratch_shapes=[
-            pltpu.VMEM((z.chunks, z.all, z.wide), BF16),
-            pltpu.VMEM((z.chunks, z.all, z.wide), BF16),
+            pltpu.VMEM((z.all, z.lanes), BF16),
+            pltpu.VMEM((z.all, z.lanes), BF16),
             pltpu.VMEM((z.chunks, z.all, z.wide + LANES), BF16),
             pltpu.VMEM((z.chunks, half, z.wide + LANES), BF16),
             pltpu.VMEM((z.chunks, half, z.wide + LANES), BF16),
@@ -555,10 +561,9 @@
             pltpu.VMEM((16, LANES), F32),
             pltpu.VMEM((z.nsp * z.message, z.pieces * z.nsp * z.tp), BF16),
             pltpu.VMEM((z.pieces * z.nsp * 8, z.nsp * z.message), BF16),
+            pltpu.VMEM((z.nsp * z.tp, z.part), F32),
             dma(2 * z.halves + 3),
-            dma(2, z.chunks, z.nchip), dma(2, z.chunks, z.nchip),
-            dma(2, z.chunks, z.nchip), dma(2, z.chunks, z.nchip),
-            dma(2, z.chunks, z.nchip), dma(2, z.chunks, z.nchip),
+            dma(2, z.nchip), dma(2, z.nchip), dma(2, z.nchip), dma(2, z.nchip), dma(2, 2), dma(2, 2),
             dma(z.chunks), dma(z.chunks),
             dma(z.chunks, z.nchip), dma(z.chunks, z.nchip),
             dma(z.nhd), dma(z.nhd),

time: 60.2 us -> 56.6 us (0.940)
  Pallas kernels: 55.9 us -> 52.2 us
    pallas_call x1, Pallas kernels: 55.9 us -> 52.2 us  [local(): pl.pallas_call(functools.partial(kernel, z), out_shape=(jax.ShapeDtypeStr...]
where the time goes in v4:
time: 56.6 us; the launch traced here: 56.2 us
  Pallas kernels  52.2 us (92%)
  local copies, waits for them, and re-layouts  2.72 us (5%)
  between operations  1.29 us (2%)
    pallas_call x1, Pallas kernels, local(): pl.pallas_call(functools.partial(kernel, z), out_shape=(jax.ShapeDtypeStr...  52.2 us
    unnamed x2, local copies, waits for them, and re-layouts  2.72 us

profile of v4, /device:TPU:1, one launch (start us, length us, event | category | flops | bytes accessed | tf_op | source)
XLA Modules:
  0.0 56.2 jit_solution(1925698540516619315)
XLA Ops:
  1.3 52.2 %span_block.1 = (bf16[3,5120]{1,0:T(4,128)(2,1)}, bf16[3,2,2,384]{3,2,1,0:T(2,128)(2,1)}) custom-call(bf16[3,2,2560]{2,1,0:T(2,128)(2,1)} %bitcast.14, bf16[3,2,2560]{2,1,0:T(2,128)(2,1)} %bitcast.15, bf16[3,2,2560]{2,1,0:T(2,128)(2,1)} %bitcast.16, s32[96]{0:T(128)} %age_ref.1, s32[1]{0:T(128)S(6)} %copy.20.history_ref, bf16[3,5120]{1,0:T(4,128)(2,1)} %bitcast.12, ...), custom_call_target="tpu_custom_call" | custom-call | tf_op jit(solution)/shard_map/span_block/pallas_call | solution.py:535
  53.5 1.4 %copy.21 = bf16[3,1,1,5120]{3,0,2,1:T(4,128)(2,1)} copy(bf16[3,1,1,5120]{3,0,2,1:T(4,128)(2,1)} %bitcast.13) | data formatting | bytes 61440
  54.9 1.3 %copy.22 = bf16[3,2,2,384]{3,2,1,0:T(2,128)(2,1)} copy(bf16[3,2,2,384]{3,2,1,0:T(2,128)(2,1)} %get-tuple-element.9) | data formatting | bytes 18432

commit v5 on v4

--- a/solution.py
+++ b/solution.py
@@ -87,12 +87,6 @@
     sib = me + 1 - 2 * core
     nchip, block = z.nchip, z.block
 
-    def peer(k):
-        return (chip + k) % nchip
-
-    def source(k):
-        return (chip + nchip - k) % nchip
-
     far, side = nchip // 2, chip % 2
 
     def place(which_chip):
@@ -251,10 +245,9 @@
     def attend(which_core, ch):
         def step(at, carry):
             rows = pl.ds(pl.multiple_of(which_core * half_rows + at * chunk, chunk), chunk)
-            stat_cols = pl.ds(z.wide, LANES)
             stats = jnp.zeros((chunk, LANES), F32)
+            outs = []
             for j in range(z.chunk_pairs):
-                near_cols = pl.ds(j * HDIM, HDIM)
                 cols = pl.ds(ch * z.wide + j * HDIM, HDIM)
                 scores = lax.dot_general(
                     g[rows, cols], k2[:, cols], (((1,), (1,)), ((), ())), preferred_element_type=F32
@@ -265,9 +258,9 @@
                 out = jnp.dot(
                     weights, jnp.concatenate([v2[:, cols], ones], axis=1), preferred_element_type=F32
                 )
-                o[ch, rows, near_cols] = out[:, :HDIM].astype(BF16)
+                outs.append(out[:, :HDIM].astype(BF16))
                 stats = jnp.where(lane == j, top, jnp.where(lane == j + 64, out[:, HDIM:], stats))
-            o[ch, rows, stat_cols] = stats.astype(BF16)
+            o[ch, rows, :] = jnp.concatenate(outs + [stats.astype(BF16)], axis=1)
             return carry
 
         if half_rows == chunk:
@@ -287,27 +280,36 @@
     def merge(ch, given):
         given.wait_recv()
         stat_cols = pl.ds(z.wide, LANES)
+        group = far * block
+        group_low = iota((group, LANES), 1) < 64
         copies = []
-        for k in list(range(1, nchip)) + [0]:
-            to = peer(k)
-            mine, rows = rows_of(core, to), chip_rows(to)
+        for across_side in (1, 0):
+            to_side = (side + across_side) % 2
+            rows = pl.ds(pl.multiple_of(to_side * group, group), group)
+            mine = pl.ds(pl.multiple_of(core * half_rows + to_side * group, group), group)
             top, total, (a, b) = merge_stats(
                 [o[ch, mine, stat_cols].astype(F32), o_in[ch, rows, stat_cols].astype(F32)]
             )
-            dst, at = (co, rows) if k else (o_got, chip_rows(chip))
-            dst[ch, at, stat_cols] = jnp.where(low, top, total).astype(BF16)
+            merged = []
             for j in range(z.chunk_pairs):
                 cols = pl.ds(j * HDIM, HDIM)
-                merged = (
+                value = (
                     o[ch, mine, cols].astype(F32) * a[:, j : j + 1]
                     + o_in[ch, rows, cols].astype(F32) * b[:, j : j + 1]
                 )
-                dst[ch, at, cols] = merged.astype(BF16)
-            if k:
-                copy = remote(co.at[ch, rows], o_got.at[ch, chip_rows(chip)], b_send.at[ch, k], b_recv.at[ch, k],
-                              to * 2 + core, my)
+                merged.append(value.astype(BF16))
+            merged.append(jnp.where(group_low, top, total).astype(BF16))
+            co[ch, rows, :] = jnp.concatenate(merged, axis=1)
+            for k in range(far):
+                if k == 0 and across_side == 0:
+                    continue
+                to = ((chip // 2 + k) % far) * 2 + to_side
+                slot = across_side * far + k
+                copy = remote(co.at[ch, chip_rows(to)], o_got.at[ch, chip_rows(chip)],
+                              b_send.at[ch, slot], b_recv.at[ch, slot], to * 2 + core, my)
                 copy.start()
                 copies.append(copy)
+        o_got[ch, chip_rows(chip), :] = co[ch, chip_rows(chip), :]
         pending.extend(copies)
         return copies
 
@@ -316,13 +318,14 @@
             copy.wait_recv()
         parts = [pl.ds(i * block, block) for i in range(nchip)]
         top, total, scales = merge_stats([o_got[ch, p, pl.ds(z.wide, LANES)].astype(F32) for p in parts])
+        done = []
         inverse = pltpu.roll(1.0 / jnp.where(low, 1.0, total), 64, 1)
         for j in range(z.chunk_pairs):
             cols = pl.ds(j * HDIM, HDIM)
             terms = [o_got[ch, p, cols].astype(F32) * s[:, j : j + 1] for p, s in zip(parts, scales)]
             summed = functools.reduce(jnp.add, terms)
-            cols = pl.ds(ch * z.wide + j * HDIM, HDIM)
-            att[rows_of(core, chip), cols] = (summed * inverse[:, j : j + 1]).astype(BF16)
+            done.append((summed * inverse[:, j : j + 1]).astype(BF16))
+        att[rows_of(core, chip), pl.ds(ch * z.wide, z.wide)] = jnp.concatenate(done, axis=1)
 
     for ch in range(z.chunks):
         attend(core, ch)

time: 56.6 us -> 57 us (level)
  no operation moved by 1% of the time
where the time goes in v5:
time: 57 us; the launch traced here: 56.7 us
  Pallas kernels  52.7 us (92%)
  local copies, waits for them, and re-layouts  2.72 us (5%)
  between operations  1.29 us (2%)
    pallas_call x1, Pallas kernels, local(): pl.pallas_call(functools.partial(kernel, z), out_shape=(jax.ShapeDtypeStr...  52.7 us
    unnamed x2, local copies, waits for them, and re-layouts  2.72 us

profile of v5, /device:TPU:1, one launch (start us, length us, event | category | flops | bytes accessed | tf_op | source)
XLA Modules:
  0.0 56.7 jit_solution(7599812005310819621)
XLA Ops:
  1.3 52.7 %span_block.1 = (bf16[3,5120]{1,0:T(4,128)(2,1)}, bf16[3,2,2,384]{3,2,1,0:T(2,128)(2,1)}) custom-call(bf16[3,2,2560]{2,1,0:T(2,128)(2,1)} %bitcast.14, bf16[3,2,2560]{2,1,0:T(2,128)(2,1)} %bitcast.15, bf16[3,2,2560]{2,1,0:T(2,128)(2,1)} %bitcast.16, s32[96]{0:T(128)} %age_ref.1, s32[1]{0:T(128)S(6)} %copy.20.history_ref, bf16[3,5120]{1,0:T(4,128)(2,1)} %bitcast.12, ...), custom_call_target="tpu_custom_call" | custom-call | tf_op jit(solution)/shard_map/span_block/pallas_call | solution.py:538
  54.0 1.4 %copy.21 = bf16[3,1,1,5120]{3,0,2,1:T(4,128)(2,1)} copy(bf16[3,1,1,5120]{3,0,2,1:T(4,128)(2,1)} %bitcast.13) | data formatting | bytes 61440
  55.4 1.3 %copy.22 = bf16[3,2,2,384]{3,2,1,0:T(2,128)(2,1)} copy(bf16[3,2,2,384]{3,2,1,0:T(2,128)(2,1)} %get-tuple-element.9) | data formatting | bytes 18432

commit v6 on v5

--- a/solution.py
+++ b/solution.py
@@ -75,9 +75,10 @@
 
 
 def kernel(
-    z, q_ref, k_ref, v_ref, age_ref, history_ref, stream_ref, gate_ref, shift_ref, scale_ref, latc_ref, gain_ref,
+    z, history_ref, q_hbm, k_hbm, v_hbm, age_hbm, stream_hbm, gate_hbm, shift_hbm, scale_hbm, latc_hbm, gain_hbm,
     ck_hbm, cv_hbm, w_hbm, hw_hbm, cw_hbm,
-    so_ref, dec_ref,
+    so_hbm, dec_hbm,
+    q_ref, k_ref, v_ref, age_ref, stream_ref, gate_ref, shift_ref, scale_ref, latc_ref, gain_ref, so_ref, dec_ref,
     g, att, o, o_in, co, o_got, k2, v2, w, hw, cw, zs, z_got, h, r_got, near, msg, tmp, pick_out, pick_in, projected,
     local_sem, z_send, z_recv, x_send, x_recv, c_send, c_recv, sib_send, sib_recv, b_send, b_recv,
     hd_send, hd_recv, e_send, e_recv, n_send, n_recv,
@@ -143,6 +144,10 @@
         copy.start()
         loads.append(copy)
 
+    load(q_hbm, q_ref)
+    load(k_hbm, k_ref)
+    load(v_hbm, v_ref)
+    load(age_hbm, age_ref)
     for half in range(z.halves):
         cols = pl.ds(half * z.lanes, z.lanes)
         load(ck_hbm.at[:, cols], k2.at[pl.ds(half * z.keys, z.cache)])
@@ -151,6 +156,12 @@
     load(w_hbm, w)
     load(hw_hbm, hw)
     load(cw_hbm, cw)
+    for src, dst in (
+        (stream_hbm, stream_ref), (gate_hbm, gate_ref), (shift_hbm, shift_ref), (scale_hbm, scale_ref),
+        (latc_hbm, latc_ref), (gain_hbm, gain_ref),
+    ):
+        load(src, dst)
+    loads[0].wait()
 
     mine_q = jnp.concatenate(packed(q_ref), axis=0).astype(BF16)
     g[rows_of(core, chip), :] = mine_q
@@ -200,6 +211,8 @@
                 copy.wait_recv()
 
     asked = Gather(g, 0)
+    for copy in loads[1:4]:
+        copy.wait()
     for ref, buf in ((k_ref, k2), (v_ref, v2)):
         for half, part in enumerate(packed(ref)):
             if z.span > z.tp:
@@ -238,7 +251,7 @@
     mask = jnp.concatenate(bounds, axis=1) > 0.0
     ones = jnp.ones((total_keys, LANES), BF16)
 
-    for copy in loads[:attention_loads]:
+    for copy in loads[4:attention_loads]:
         copy.wait()
     asked.relay()
 
@@ -454,6 +467,7 @@
     tmp[past : past + z.frames, 0:cells] = patch[0 : z.frames]
     msg[...] = tmp[...].astype(BF16)
 
+    written = [pltpu.make_async_copy(so_ref, so_hbm, local_sem.at[0])]
     order = [(dr, dc) for dr in (-1, 0, 1) for dc in (-1, 0, 1) if (dr, dc) != (0, 0)]
 
     def halo(dr, dc):
@@ -467,6 +481,9 @@
             halo(dr, dc).start()
 
     near[4] = msg[...]
+    written[0].start()
+    for copy in pending:
+        copy.wait_send()
     for dr, dc in order:
 
         @pl.when(inside(dr, dc))
@@ -507,8 +524,6 @@
             jnp.dot(wide_taps, cw[pl.ds(u * taps, LANES), :], preferred_element_type=F32)
             + jnp.dot(rest_taps, cw[pl.ds(u * taps + LANES, taps - LANES), :], preferred_element_type=F32)
         )
-    for copy in pending:
-        copy.wait_send()
     gain = gain_ref[...][None, :]
     decoded = []
     for cell in range(4):
@@ -521,6 +536,21 @@
         for i in range(2):
             pair_of = [decoded[i * 2 + j][f : f + 1] for j in range(2)]
             dec_ref[f, i] = jnp.concatenate(pair_of, axis=0).astype(BF16)
+    written.append(pltpu.make_async_copy(dec_ref, dec_hbm, local_sem.at[1]))
+    written[1].start()
+    for copy in written:
+        copy.wait()
+
+
+def hand_over(out_hbm, dec_hbm, so_hbm, do_hbm, sems):
+    copies = [
+        pltpu.make_async_copy(out_hbm, so_hbm, sems.at[0]),
+        pltpu.make_async_copy(dec_hbm, do_hbm, sems.at[1]),
+    ]
+    for copy in copies:
+        copy.start()
+    for copy in copies:
+        copy.wait()
 
 
 def local(
@@ -531,19 +561,24 @@
     out_weight, head_weight = out_weight.T, head_weight.T
     z = Sizes(mesh, queries, cache_k, out_weight)
     model, chan = z.model, conv_weight.shape[1]
-    vmem = pl.BlockSpec(memory_space=pltpu.VMEM)
     hbm = pl.BlockSpec(memory_space=pl.ANY)
     half = z.all // 2
     dma = lambda *shape: pltpu.SemaphoreType.DMA(shape)
+    shapes = (
+        jax.ShapeDtypeStruct((z.frames, model), BF16),
+        jax.ShapeDtypeStruct((z.frames, 2, 2, chan), BF16),
+    )
+    small = (
+        queries, span_k, span_v, cache_age, stream.reshape(z.frames, model),
+        attn_gate[None], head_shift[None], head_scale[None], latent_cache, rms_gain,
+    )
     out, dec = pl.pallas_call(
         functools.partial(kernel, z),
-        out_shape=(
-            jax.ShapeDtypeStruct((z.frames, model), BF16),
-            jax.ShapeDtypeStruct((z.frames, 2, 2, chan), BF16),
-        ),
-        in_specs=[vmem] * 4 + [pl.BlockSpec(memory_space=pltpu.SMEM)] + [vmem] * 6 + [hbm] * 5,
-        out_specs=(vmem, vmem),
+        out_shape=shapes,
+        in_specs=[pl.BlockSpec(memory_space=pltpu.SMEM)] + [hbm] * 15,
+        out_specs=(hbm, hbm),
         scratch_shapes=[
+            *[pltpu.VMEM(t.shape, t.dtype) for t in (*small, *shapes)],
             pltpu.VMEM((z.all, z.lanes), BF16),
             pltpu.VMEM((z.all, z.lanes), BF16),
             pltpu.VMEM((z.chunks, z.all, z.wide + LANES), BF16),
@@ -565,7 +600,7 @@
             pltpu.VMEM((z.nsp * z.message, z.pieces * z.nsp * z.tp), BF16),
             pltpu.VMEM((z.pieces * z.nsp * 8, z.nsp * z.message), BF16),
             pltpu.VMEM((z.nsp * z.tp, z.part), F32),
-            dma(2 * z.halves + 3),
+            dma(2 * z.halves + 13),
             dma(2, z.nchip), dma(2, z.nchip), dma(2, z.nchip), dma(2, z.nchip), dma(2, 2), dma(2, 2),
             dma(z.chunks), dma(z.chunks),
             dma(z.chunks, z.nchip), dma(z.chunks, z.nchip),
@@ -578,10 +613,17 @@
         ),
         name="span_block",
     )(
-        queries, span_k, span_v, cache_age, history, stream.reshape(z.frames, model),
-        attn_gate[None], head_shift[None], head_scale[None], latent_cache, rms_gain,
-        cache_k, cache_v, out_weight, head_weight, conv_weight,
+        history, *small, cache_k, cache_v, out_weight, head_weight, conv_weight,
     )
+    out, dec = pl.pallas_call(
+        hand_over,
+        out_shape=shapes,
+        in_specs=[hbm] * 2,
+        out_specs=(hbm, hbm),
+        scratch_shapes=[dma(2)],
+        compiler_params=pltpu.CompilerParams(vmem_limit_bytes=63 * 1024 * 1024),
+        name="hand_over",
+    )(out, dec)
     return out.reshape(stream.shape), dec
 
 

time: 57 us -> 55.9 us (0.981)
  local copies, waits for them, and re-layouts: 2.72 us -> 0 us
  Pallas kernels: 52.7 us -> 54.5 us
    unnamed x2 -> x0, local copies, waits for them, and re-layouts: 2.72 us -> none
    pallas_call x1 -> x2, Pallas kernels: 52.7 us -> 54.5 us  [the longest x1 51.9 us: local(): pl.pallas_call(functools.partial(kernel, z), out_shape=shapes, in_specs=[...]
where the time goes in v6:
time: 55.9 us; the launch traced here: 55.8 us
  Pallas kernels  54.5 us (97%)
  between operations  1.29 us (2%)
    pallas_call x1, Pallas kernels, local(): pl.pallas_call(functools.partial(kernel, z), out_shape=shapes, in_specs=[...  51.9 us
    pallas_call x1, Pallas kernels, local(): pl.pallas_call(hand_over, out_shape=shapes, in_specs=[hbm] * 2, out_specs...  2.64 us

profile of v6, /device:TPU:1, one launch (start us, length us, event | category | flops | bytes accessed | tf_op | source)
XLA Modules:
  0.0 55.8 jit_solution(10862668124961843100)
XLA Ops:
  1.3 51.9 %span_block.1 = (bf16[3,5120]{1,0:T(4,128)(2,1)}, bf16[3,2,2,384]{3,2,1,0:T(2,128)(2,1)}) custom-call(s32[1]{0:T(128)S(6)} %copy.18.history_ref, bf16[3,2,2560]{2,1,0:T(2,128)(2,1)} %bitcast.13, bf16[3,2,2560]{2,1,0:T(2,128)(2,1)} %bitcast.14, bf16[3,2,2560]{2,1,0:T(2,128)(2,1)} %bitcast.15, s32[96]{0:T(128)} %age_hbm.1, bf16[3,5120]{1,0:T(4,128)(2,1)} %bitcast.12, ...), custom_call_target="tpu_custom_call" | custom-call | tf_op jit(solution)/shard_map/span_block/pallas_call | solution.py:575
  53.2 2.6 %hand_over.1 = (bf16[3,5120]{1,0:T(4,128)(2,1)}, bf16[3,2,2,384]{3,2,1,0:T(2,128)(2,1)}) custom-call(bf16[3,5120]{1,0:T(4,128)(2,1)} %get-tuple-element.6.out_hbm, bf16[3,2,2,384]{3,2,1,0:T(2,128)(2,1)} %get-tuple-element.7.dec_hbm), custom_call_target="tpu_custom_call" | custom-call | tf_op jit(solution)/shard_map/hand_over/pallas_call | solution.py:618

commit v7 on v6

--- a/solution.py
+++ b/solution.py
@@ -46,6 +46,7 @@
         self.pieces = -(-self.part // LANES)
         self.message = up(self.pieces * self.slot, 16)
         self.model = self.part * self.nsp
+        self.direct = self.nsp * self.nhd <= 64
 
     def slots(self):
         for f in range(self.frames):
@@ -115,9 +116,13 @@
     near[...] = jnp.zeros_like(near)
 
     barrier = pltpu.get_barrier_semaphore()
+    if z.direct:
+        for k in range(z.nsp, z.nsp * z.nhd):
+            there = ((me + k) % z.nsp, (my + k // z.nsp) % z.nhd)
+            pl.semaphore_signal(barrier, inc=1, device_id=there, device_id_type=MESH)
     for k in range(1, z.nsp):
         pl.semaphore_signal(barrier, inc=1, device_id=((me + k) % z.nsp, my), device_id_type=MESH)
-    for k in range(1, z.nhd):
+    for k in range(1, 1 if z.direct else z.nhd):
         pl.semaphore_signal(barrier, inc=1, device_id=(me, (my + k) % z.nhd), device_id_type=MESH)
 
     def inside(dr, dc):
@@ -128,8 +133,8 @@
                 ok = here if ok is None else ok & here
         return ok
 
-    greeted = z.nsp - 1 + z.nhd - 1
-    for dr in (-1, 1):
+    greeted = z.nsp * z.nhd - 1 if z.direct else z.nsp - 1 + z.nhd - 1
+    for dr in () if z.direct else (-1, 1):
         for dc in (-1, 1):
 
             @pl.when(inside(dr, dc))
@@ -387,32 +392,50 @@
     for owner in range(z.nhd):
         zs[owner] = moved[:, owner * LANES : (owner + 1) * LANES]
 
-    swaps = []
-    for k in range(1, z.nhd):
-        to = (my + k) % z.nhd
-        copy = remote(zs.at[to], z_got.at[my], hd_send.at[k], hd_recv.at[k], me, to)
-        copy.start()
-        swaps.append(copy)
-    summed = zs[my].astype(F32)
-    for k in range(1, z.nhd):
-        swaps[k - 1].wait_recv()
-        summed = summed + z_got[(my + z.nhd - k) % z.nhd].astype(F32)
-    h[...] = summed.astype(BF16)
-
     def message_rows(at):
         return pl.ds(pl.multiple_of(at * z.message, z.message), z.message)
 
-    spread = []
-    for k in range(1, z.nsp):
-        to = (me + k) % z.nsp
-        copy = remote(h.at[message_rows(to)], r_got.at[message_rows(me)], e_send.at[k], e_recv.at[k], to, my)
-        copy.start()
-        spread.append(copy)
-    r_got[message_rows(me), :] = h[message_rows(me), :]
-    pending.extend(swaps)
-    pending.extend(spread)
-    for copy in spread:
-        copy.wait_recv()
+    if z.direct:
+        spread = []
+        for dh in range(z.nhd - 1, -1, -1):
+            for ds in range(z.nsp):
+                if dh or ds:
+                    to_hd, to = (my + dh) % z.nhd, (me + ds) % z.nsp
+                    slot = dh * z.nsp + ds
+                    copy = remote(zs.at[to_hd, message_rows(to)], z_got.at[my, message_rows(me)],
+                                  e_send.at[slot], e_recv.at[slot], to, to_hd)
+                    copy.start()
+                    spread.append(copy)
+        z_got[my, message_rows(me), :] = zs[my, message_rows(me), :]
+        pending.extend(spread)
+        for copy in spread:
+            copy.wait_recv()
+        summed = functools.reduce(jnp.add, [z_got[i].astype(F32) for i in range(z.nhd)])
+        r_got[...] = summed.astype(BF16)
+    else:
+        swaps = []
+        for k in range(1, z.nhd):
+            to = (my + k) % z.nhd
+            copy = remote(zs.at[to], z_got.at[my], hd_send.at[k], hd_recv.at[k], me, to)
+            copy.start()
+            swaps.append(copy)
+        summed = zs[my].astype(F32)
+        for k in range(1, z.nhd):
+            swaps[k - 1].wait_recv()
+            summed = summed + z_got[(my + z.nhd - k) % z.nhd].astype(F32)
+        h[...] = summed.astype(BF16)
+
+        spread = []
+        for k in range(1, z.nsp):
+            to = (me + k) % z.nsp
+            copy = remote(h.at[message_rows(to)], r_got.at[message_rows(me)], e_send.at[k], e_recv.at[k], to, my)
+            copy.start()
+            spread.append(copy)
+        r_got[message_rows(me), :] = h[message_rows(me), :]
+        pending.extend(swaps)
+        pending.extend(spread)
+        for copy in spread:
+            copy.wait_recv()
 
     picked = jnp.dot(pick_in[...], r_got[...], preferred_element_type=F32)
     by_piece = [picked[i * to_rows : (i + 1) * to_rows] for i in range(z.pieces)]
@@ -563,6 +586,7 @@
     model, chan = z.model, conv_weight.shape[1]
     hbm = pl.BlockSpec(memory_space=pl.ANY)
     half = z.all // 2
+    spread = z.nsp * z.nhd if z.direct else z.nsp
     dma = lambda *shape: pltpu.SemaphoreType.DMA(shape)
     shapes = (
         jax.ShapeDtypeStruct((z.frames, model), BF16),
@@ -605,7 +629,7 @@
             dma(z.chunks), dma(z.chunks),
             dma(z.chunks, z.nchip), dma(z.chunks, z.nchip),
             dma(z.nhd), dma(z.nhd),
-            dma(z.nsp), dma(z.nsp),
+            dma(spread), dma(spread),
             dma(9), dma(9),
         ],
         compiler_params=pltpu.CompilerParams(

time: 55.9 us -> 54.1 us (0.968)
  Pallas kernels: 54.5 us -> 52.7 us
    pallas_call x1, Pallas kernels: 51.9 us -> 50 us  [local(): pl.pallas_call(functools.partial(kernel, z), out_shape=shapes, in_specs=[...]
where the time goes in v7:
time: 54.1 us; the launch traced here: 54 us
  Pallas kernels  52.7 us (97%)
  between operations  1.29 us (2%)
    pallas_call x1, Pallas kernels, local(): pl.pallas_call(functools.partial(kernel, z), out_shape=shapes, in_specs=[...  50 us
    pallas_call x1, Pallas kernels, local(): pl.pallas_call(hand_over, out_shape=shapes, in_specs=[hbm] * 2, out_specs...  2.64 us

profile of v7, /device:TPU:1, one launch (start us, length us, event | category | flops | bytes accessed | tf_op | source)
XLA Modules:
  0.0 54.0 jit_solution(2381628978612927206)
XLA Ops:
  1.3 50.0 %span_block.1 = (bf16[3,5120]{1,0:T(4,128)(2,1)}, bf16[3,2,2,384]{3,2,1,0:T(2,128)(2,1)}) custom-call(s32[1]{0:T(128)S(6)} %copy.18.history_ref, bf16[3,2,2560]{2,1,0:T(2,128)(2,1)} %bitcast.13, bf16[3,2,2560]{2,1,0:T(2,128)(2,1)} %bitcast.14, bf16[3,2,2560]{2,1,0:T(2,128)(2,1)} %bitcast.15, s32[96]{0:T(128)} %age_hbm.1, bf16[3,5120]{1,0:T(4,128)(2,1)} %bitcast.12, ...), custom_call_target="tpu_custom_call" | custom-call | tf_op jit(solution)/shard_map/span_block/pallas_call | solution.py:599
  51.3 2.6 %hand_over.1 = (bf16[3,5120]{1,0:T(4,128)(2,1)}, bf16[3,2,2,384]{3,2,1,0:T(2,128)(2,1)}) custom-call(bf16[3,5120]{1,0:T(4,128)(2,1)} %get-tuple-element.6.out_hbm, bf16[3,2,2,384]{3,2,1,0:T(2,128)(2,1)} %get-tuple-element.7.dec_hbm), custom_call_target="tpu_custom_call" | custom-call | tf_op jit(solution)/shard_map/hand_over/pallas_call | solution.py:642
